TPU v7x, 256 devices: a whole 4x4x8 slice. The times are simulated.
256 devices in a mesh: dp: 2 (over core), expert: 16 (over x, y), tensor: 8 (over z).
Axes of the slice: x: 4, y: 4, z: 8, core: 2. Of those that a mesh axis runs over, the one named last changes fastest.
Arguments:
- layer_input: bfloat16 [4096, 3584], P(('dp', 'expert'), 'tensor'), may hold values from -6 to 6
- cotangent: bfloat16 [4096, 3584], P(('dp', 'expert'), 'tensor'), may hold values from -1.25 to 1.25
- route_probs: float32 [4096, 2], P(('dp', 'expert')), may hold values from 0.1 to 1
- routes: int32 [4096, 2], P(('dp', 'expert')), may hold values from 0 to 15, all different within a row; in each aligned block of 128 rows (0 to 127, 128 to 255, ...) at most 20 rows name the same one
- shared_gate: bfloat16 [3584, 2432], P('dp', 'tensor'), may hold values from -0.09375 to 0.09375
- shared_up: bfloat16 [3584, 2432], P('dp', 'tensor'), may hold values from -0.09375 to 0.09375
- shared_down: bfloat16 [2432, 3584], P('tensor', 'dp'), may hold values from -0.125 to 0.125
- routed_gate: bfloat16 [16, 3584, 2432], P('expert', 'dp', 'tensor'), may hold values from -0.09375 to 0.09375
- routed_up: bfloat16 [16, 3584, 2432], P('expert', 'dp', 'tensor'), may hold values from -0.09375 to 0.09375
- routed_down: bfloat16 [16, 2432, 3584], P('expert', 'tensor', 'dp'), may hold values from -0.125 to 0.125
Outputs:
- input_grad: bfloat16 [4096, 3584], P(('dp', 'expert'), 'tensor')
- prob_grad: float32 [4096, 2], P(('dp', 'expert'))
- grad_gate: bfloat16 [3584, 2432], P(('dp', 'expert'), 'tensor')
- grad_up: bfloat16 [3584, 2432], P(('dp', 'expert'), 'tensor')
- grad_down: bfloat16 [2432, 3584], P('tensor', ('dp', 'expert'))
- delta_gate: bfloat16 [16, 3584, 2432], P('expert', 'dp', 'tensor')
- delta_up: bfloat16 [16, 3584, 2432], P('expert', 'dp', 'tensor')
- delta_down: bfloat16 [16, 2432, 3584], P('expert', 'tensor', 'dp')
Inputs may be any that keep to these rules, and one draw needn't show every extreme that they name: `routes`: each token names 2 different experts. Among the 128 rows of one block, no expert is named more than 20 times, and in every draw some expert is named exactly 20 times in some block.
All inputs are finite; a program needn't handle non-finite values.
Results may differ from a plain program's by a relative error of at most 0.022.
Values may be sent and summed in bfloat16 or wider, within the bound.
No kernel may reach another device: no remote copies, remote signals or barrier semaphores. Data moves between devices by JAX's collectives and lax.ppermute only.
A program may use at most 192 MiB of HBM per device.

v0:
```python
import functools

import jax
import jax.numpy as jnp
from jax import lax
from jax.experimental import pallas as pl
from jax.experimental.pallas import tpu as pltpu
from jax.sharding import PartitionSpec as P

TOP = 2
TILE = 16
LANES = 128
VMEM_LIMIT = 56 * 1024 * 1024
F32 = jnp.float32
BF16 = jnp.bfloat16


def product(spec, left, right):
    return jnp.einsum(spec, left, right, preferred_element_type=F32)


def swap(values):
    return lax.ppermute(values, "dp", [(0, 1), (1, 0)])


def ring(values, shift):
    size = lax.axis_size("tensor")
    return lax.ppermute(values, "tensor", [(i, (i + shift) % size) for i in range(size)])


def single_ring(chunk, steps, state=None):
    size = lax.axis_size("tensor")
    right, left = state or (chunk, chunk)
    pieces = []
    for step in steps:
        right = ring(right, 1)
        pieces.append((right, size - step))
        if step < size - step:
            left = ring(left, -1)
            pieces.append((left, step))
    return pieces, (right, left)


def halves(values, axis):
    half = values.shape[axis] // 2
    index = lax.axis_index("dp")
    return (
        lax.dynamic_slice_in_dim(values, index * half, half, axis),
        lax.dynamic_slice_in_dim(values, (1 - index) * half, half, axis),
    )


def sigmoid_parts(pre_gate):
    sigmoid = 1.0 / (1.0 + jnp.exp(jnp.minimum(-pre_gate, 80.0)))
    return pre_gate * sigmoid, sigmoid * (1.0 + pre_gate * (1.0 - sigmoid))


def select(mask):
    return jnp.where(mask, 1.0, 0.0).astype(BF16)


def contract(left, right, left_dim, right_dim):
    return lax.dot_general(
        left, right, (((left_dim,), (right_dim,)), ((), ())), preferred_element_type=F32
    )


def costs(micros):
    return pl.CostEstimate(flops=1, bytes_accessed=int(micros * 3.5e6), transcendentals=0)


def shape_of(shape, dtype=BF16):
    return jax.ShapeDtypeStruct(shape, dtype)


def params():
    return pltpu.CompilerParams(
        dimension_semantics=("arbitrary",), vmem_limit_bytes=VMEM_LIMIT
    )


def dispatch_kernel(capacity, routes_ref, probs_ref, both_ref, folded_ref, places_ref):
    tokens = routes_ref.shape[1]
    main, wide = folded_ref.shape
    feats = both_ref.shape[0]
    left = capacity - TILE
    quarters = TILE // left
    piece = feats // quarters
    lane = lax.broadcasted_iota(jnp.int32, (tokens, LANES), 1)
    row = lax.broadcasted_iota(jnp.int32, (tokens, tokens), 0)
    column = lax.broadcasted_iota(jnp.int32, (tokens, tokens), 1)

    def column_of(ref, k):
        return jnp.broadcast_to(ref[k : k + 1, :].astype(F32), (tokens, tokens)).T

    routed = [column_of(routes_ref, k).astype(jnp.int32) for k in range(TOP)]
    probs = [column_of(probs_ref, k).astype(BF16).astype(F32)[:, :LANES] for k in range(TOP)]
    named = [lane == routed[k][:, :LANES] for k in range(TOP)]
    earlier = jnp.dot(
        select(row > column), select(named[0] | named[1]), preferred_element_type=F32
    )
    slot = lax.broadcasted_iota(jnp.int32, (tokens, main), 1)
    near, far = [], []
    for k in range(TOP):
        rank = jnp.sum(jnp.where(named[k], earlier, 0.0), axis=1, keepdims=True).astype(jnp.int32)
        first = routed[k][:, :1] * TILE + rank
        near.append(jnp.where(rank < TILE, first, -main))
        far.append(jnp.where(rank < TILE, -main, first - TILE))
    for k in range(TOP):
        places_ref[:, k : k + 1] = near[k]
        places_ref[:, TOP + k : TOP + k + 1] = far[k]
    near = [select(slot == place) for place in near]
    folded_ref[:, :feats] = contract(near[0] + near[1], both_ref[...], 0, 1).astype(BF16)
    rest = jnp.zeros((main, piece), F32)
    for quarter in range(quarters):
        picked = [select(slot == place + quarter * left) for place in far]
        rest += contract(
            picked[0] + picked[1], both_ref[quarter * piece : (quarter + 1) * piece, :], 0, 1
        )
    folded_ref[:, feats : feats + piece] = rest.astype(BF16)
    scales = jnp.zeros((main, LANES), F32)
    for k in range(TOP):
        scales += contract(near[k], jnp.where(lane == 0, probs[k], 0.0).astype(BF16), 0, 0)
        scales += contract(
            select(slot == far[k]), jnp.where(lane == 1, probs[k], 0.0).astype(BF16), 0, 0
        )
    folded_ref[:, feats + piece :] = scales[:, : wide - feats - piece].astype(BF16)


def dispatch(routes, probs, both, experts, capacity):
    feats, tokens = both.shape
    wide = feats + feats * (capacity - TILE) // TILE
    wide = (wide // LANES + 1) * LANES
    return pl.pallas_call(
        functools.partial(dispatch_kernel, capacity),
        out_shape=[
            shape_of((experts * TILE, wide)),
            shape_of((tokens, 2 * TOP), jnp.int32),
        ],
        compiler_params=pltpu.CompilerParams(vmem_limit_bytes=VMEM_LIMIT),
        cost_estimate=costs(3),
    )(routes, probs, both)


def dense_kernel(distances, coords_ref, *refs):
    pieces = refs[: len(distances)]
    (
        gate_own_ref,
        gate_other_ref,
        up_own_ref,
        up_other_ref,
        down_own_ref,
        down_other_ref,
        own_ref,
        backs_ref,
        hidden_ref,
        pair_terms_ref,
        down_terms_ref,
        rows,
        arrivals,
        pre,
        from_down,
    ) = refs[len(distances) :]
    step = pl.program_id(0)
    size, wide, tokens = rows.shape
    parts = size // 4
    feats = wide // 2
    units = hidden_ref.shape[0]
    block = parts * feats
    place = lax.rem(coords_ref[1] * 2 + jnp.where(step < 4, step, step - 2), 4)

    @pl.when(step == 0)
    def _():
        for ref, distance in zip(pieces, distances):
            origin = lax.rem(coords_ref[0] + distance, size)
            pltpu.make_async_copy(ref, rows.at[origin], arrivals.at[origin]).start()
        pre[...] = jnp.zeros_like(pre)
        from_down[...] = jnp.zeros_like(from_down)

    @pl.when(step < 4)
    def _():
        for part in range(parts):
            origin = place * parts + part
            pltpu.make_async_copy(pieces[0], rows.at[origin], arrivals.at[origin]).wait()

    @pl.when(step < 2)
    def _():
        own_ref[...] = rows[pl.ds(place * parts, parts)]

    rows_in = rows[pl.ds(place * parts, parts), :feats, :].reshape(block, tokens)
    rows_out = rows[pl.ds(place * parts, parts), feats:, :].reshape(block, tokens)

    def forward(gate_ref, up_ref, down_ref):
        pair = jnp.concatenate([gate_ref[...], up_ref[...]], axis=0)
        pre[...] += jnp.dot(pair, rows_in, preferred_element_type=F32)
        from_down[...] += jnp.dot(down_ref[...], rows_out, preferred_element_type=F32)

    @pl.when(step < 2)
    def _():
        forward(gate_own_ref, up_own_ref, down_own_ref)

    @pl.when((step >= 2) & (step < 4))
    def _():
        forward(gate_other_ref, up_other_ref, down_other_ref)

    @pl.when(step == 3)
    def _():
        act, slope = sigmoid_parts(pre[:units])
        raised = pre[units:]
        back = from_down[...]
        hidden_ref[...] = (act * raised).astype(BF16)
        backs_ref[:units] = (back * raised * slope).astype(BF16)
        backs_ref[units:] = (back * act).astype(BF16)

    @pl.when(step >= 4)
    def _():
        backs = contract(rows_in, backs_ref[...], 1, 1).astype(BF16)
        down = contract(rows_out, hidden_ref[...], 1, 1).astype(BF16)
        empty = pair_terms_ref.shape[1] - 2 * units
        pair_terms_ref[...] = jnp.concatenate([backs, jnp.zeros((block, empty), BF16)], axis=1)
        empty = down_terms_ref.shape[1] - units
        down_terms_ref[...] = jnp.concatenate([down, jnp.zeros((block, empty), BF16)], axis=1)


def lane_up(count):
    return -(-count // LANES) * LANES


def dense_forward(pieces, coords, gates, ups, downs):
    size = lax.axis_size("tensor")
    wide, tokens = pieces[0][0].shape
    units, half_width = downs[0].shape
    parts = size // 4
    block = parts * wide // 2
    own = lambda i, c: (0, jnp.minimum(i, 1))
    other = lambda i, c: (0, jnp.clip(i - 2, 0, 1))
    whole = lambda shape: pl.BlockSpec(shape, lambda i, c: (0, 0))
    term = lambda lanes: pl.BlockSpec((block, lanes), lambda i, c: (jnp.maximum(i - 4, 0), 0))
    return pl.pallas_call(
        functools.partial(dense_kernel, [piece[1] for piece in pieces]),
        grid_spec=pltpu.PrefetchScalarGridSpec(
            num_scalar_prefetch=1,
            grid=(6,),
            in_specs=[pl.BlockSpec(memory_space=pl.ANY)] * len(pieces)
            + [pl.BlockSpec((units, block), own), pl.BlockSpec((units, block), other)] * 3,
            out_specs=[
                pl.BlockSpec((parts, wide, tokens), lambda i, c: (jnp.minimum(i, 1), 0, 0)),
                whole((2 * units, tokens)),
                whole((units, tokens)),
                term(lane_up(2 * units)),
                term(lane_up(units)),
            ],
            scratch_shapes=[
                pltpu.VMEM((size, wide, tokens), BF16),
                pltpu.SemaphoreType.DMA((size,)),
                pltpu.VMEM((2 * units, tokens), F32),
                pltpu.VMEM((units, tokens), F32),
            ],
        ),
        out_shape=[
            shape_of((2 * parts, wide, tokens)),
            shape_of((2 * units, tokens)),
            shape_of((units, tokens)),
            shape_of((half_width, lane_up(2 * units))),
            shape_of((half_width, lane_up(units))),
        ],
        compiler_params=params(),
        cost_estimate=costs(10),
    )(coords, *[piece[0] for piece in pieces], *gates, *ups, *downs)


def terms_kernel(both_ref, backs_ref, hidden_ref, pair_arrived_ref, down_arrived_ref, terms_ref):
    parts, wide, tokens = both_ref.shape
    feats = wide // 2
    units = hidden_ref.shape[0]
    block = parts * feats
    first = pair_arrived_ref.shape[1]
    rows_in = both_ref[:, :feats, :].reshape(block, tokens)
    rows_out = both_ref[:, feats:, :].reshape(block, tokens)
    backs = contract(rows_in, backs_ref[...], 1, 1) + pair_arrived_ref[:, : 2 * units].astype(F32)
    down = contract(rows_out, hidden_ref[...], 1, 1) + down_arrived_ref[:, :units].astype(F32)
    empty = jnp.zeros((block, first - 2 * units), BF16)
    terms_ref[:, :first] = jnp.concatenate([backs.astype(BF16), empty], axis=1)
    empty = jnp.zeros((block, terms_ref.shape[1] - first - units), BF16)
    terms_ref[:, first:] = jnp.concatenate([down.astype(BF16), empty], axis=1)


def dense_terms(own, backs, hidden, pair_arrived, down_arrived):
    size, wide, tokens = own.shape
    units = hidden.shape[0]
    parts = size // 2
    block = parts * wide // 2
    half_width, first = pair_arrived.shape
    second = down_arrived.shape[1]
    whole = lambda shape: pl.BlockSpec(shape, lambda i: (0, 0))
    tall = lambda lanes: pl.BlockSpec((block, lanes), lambda i: (i, 0))
    return pl.pallas_call(
        terms_kernel,
        grid=(2,),
        in_specs=[
            pl.BlockSpec((parts, wide, tokens), lambda i: (i, 0, 0)),
            whole((2 * units, tokens)),
            whole((units, tokens)),
            tall(first),
            tall(second),
        ],
        out_specs=tall(first + second),
        out_shape=shape_of((half_width, first + second)),
        compiler_params=params(),
        cost_estimate=costs(5),
    )(own, backs, hidden, pair_arrived, down_arrived)


def expert_kernel(
    capacity,
    coords_ref,
    slices_ref,
    gate_own_ref,
    gate_other_ref,
    up_own_ref,
    up_other_ref,
    down_own_ref,
    down_other_ref,
    rows_in_ref,
    scaled_out_ref,
    sent_ref,
    hidden_ref,
    backs_ref,
    pre,
    from_down,
    folded,
    scale,
):
    step = pl.program_id(0)
    quarters = pl.num_programs(0) // 2
    pair, main, _ = slices_ref.shape
    block = gate_own_ref.shape[1]
    units = hidden_ref.shape[1]
    feats = block // pair
    piece = feats * 2 // quarters
    rest = rows_in_ref.shape[0] - main
    left = capacity - TILE
    owned = lax.rem(step, quarters) < quarters // 2
    place = lax.rem(coords_ref[1] * (quarters // 2) + step, quarters)

    source = lax.broadcasted_iota(jnp.int32, (main, rest), 1)
    target = lax.broadcasted_iota(jnp.int32, (main, rest), 0)

    def fold(quarter):
        return select(target == source // left * TILE + quarter * left + source % left)

    @pl.when(step == 0)
    def _():
        pre[...] = jnp.zeros_like(pre)
        from_down[...] = jnp.zeros_like(from_down)
        folded[...] = jnp.zeros_like(folded)

    def forward(gate_ref, up_ref, down_ref):
        pair_rows = jnp.concatenate([gate_ref[...], up_ref[...]], axis=0)
        parts = [slices_ref[part] for part in range(pair)]

        @pl.when(step == 0)
        def _():
            scales = parts[0][:, 2 * feats + piece :]
            scale[:main] = scales[:, 0:1].astype(F32)
            scale[main:] = contract(fold(0), scales, 0, 0)[:, 1:2]

        rows_in_ref[:main] = jnp.concatenate([part[:, :feats] for part in parts], axis=1)
        rows_out = jnp.concatenate([part[:, feats : 2 * feats] for part in parts], axis=1)
        beside = jnp.concatenate(
            [part[:, 2 * feats : 2 * feats + piece] for part in parts], axis=1
        )
        spread = [contract(fold(quarter), beside, 0, 0).astype(BF16) for quarter in range(quarters)]
        half = quarters // 2

        def unfolded(which):
            return jnp.concatenate(
                [
                    spread[which * half + quarter][:, part * piece : (part + 1) * piece]
                    for part in range(pair)
                    for quarter in range(half)
                ],
                axis=1,
            )

        rows_in_ref[main:] = unfolded(0)
        rows_out = jnp.concatenate([rows_out, unfolded(1)], axis=0)
        scaled_out_ref[...] = (scale[...] * rows_out.astype(F32)).astype(BF16)
        pre[...] += contract(rows_in_ref[...], pair_rows, 1, 1)
        from_down[...] += contract(rows_out, down_ref[...], 1, 1)

    @pl.when((step < quarters) & owned)
    def _():
        forward(gate_own_ref, up_own_ref, down_own_ref)

    @pl.when((step < quarters) & jnp.logical_not(owned))
    def _():
        forward(gate_other_ref, up_other_ref, down_other_ref)

    @pl.when(step == quarters - 1)
    def _():
        back = from_down[...]
        act, slope = sigmoid_parts(pre[:, :units])
        raised = pre[:, units:]
        hidden = (act * raised).astype(BF16)
        hidden_ref[...] = hidden
        scaled = scale[...] * back
        backs_ref[...] = jnp.concatenate(
            [(scaled * raised * slope).astype(BF16), (scaled * act).astype(BF16)], axis=1
        )
        probe = jnp.sum(hidden.astype(F32) * back, axis=1, keepdims=True)
        high = probe.astype(BF16).astype(F32)
        low = probe - high
        lane = lax.broadcasted_iota(jnp.int32, (main, LANES), 1)
        beside = jnp.where(lane == 0, high[:main], jnp.where(lane == 1, low[:main], 0.0))
        lane = lax.broadcasted_iota(jnp.int32, (rest, LANES), 1)
        after = jnp.where(lane == 2, high[main:], jnp.where(lane == 3, low[main:], 0.0))
        after = jnp.dot(fold(0), after.astype(BF16), preferred_element_type=F32)
        sent_ref[:, sent_ref.shape[1] - LANES :] = (beside + after).astype(BF16)

    def backward(gate_ref, up_ref):
        pair_rows = jnp.concatenate([gate_ref[...], up_ref[...]], axis=0)
        rows = jnp.dot(backs_ref[...], pair_rows, preferred_element_type=F32).astype(BF16)
        sent_ref[:, pl.ds(pl.multiple_of(place * block, LANES), block)] = rows[:main]
        folded[...] += jnp.dot(fold(place), rows[main:], preferred_element_type=F32)

    @pl.when((step >= quarters) & owned)
    def _():
        backward(gate_own_ref, up_own_ref)

    @pl.when((step >= quarters) & jnp.logical_not(owned))
    def _():
        backward(gate_other_ref, up_other_ref)

    @pl.when(step == 2 * quarters - 1)
    def _():
        sent_ref[:, quarters * block : (quarters + 1) * block] = folded[...].astype(BF16)


def expert_rows(slices, coords, gates, ups, downs, experts, capacity):
    size, main, wide = slices.shape
    units, half_width = downs[0].shape
    width = 2 * half_width
    quarters = TILE // (capacity - TILE)
    block = width // quarters
    rows = experts * capacity
    whole = lambda shape: pl.BlockSpec(shape, lambda i, c: (0, 0))
    last = quarters // 2 - 1

    def early(i, c):
        return (0, lax.rem(c[1] * (quarters // 2) + jnp.minimum(i, quarters - 1), quarters))

    def own(i, c):
        return (0, jnp.minimum(lax.rem(i, quarters), last))

    def other(i, c):
        return (0, jnp.maximum(lax.rem(i, quarters), last + 1) - last - 1)

    def own_once(i, c):
        return (0, jnp.minimum(i, last))

    def other_once(i, c):
        return (0, jnp.clip(i - last - 1, 0, last))

    return pl.pallas_call(
        functools.partial(expert_kernel, capacity),
        grid_spec=pltpu.PrefetchScalarGridSpec(
            num_scalar_prefetch=1,
            grid=(2 * quarters,),
            in_specs=[pl.BlockSpec((size // quarters, main, wide), lambda i, c: early(i, c)[::-1] + (0,))]
            + [pl.BlockSpec((units, block), own), pl.BlockSpec((units, block), other)] * 2
            + [pl.BlockSpec((units, block), own_once), pl.BlockSpec((units, block), other_once)],
            out_specs=[
                pl.BlockSpec((rows, block), early),
                pl.BlockSpec((rows, block), early),
                whole((main, width + block + LANES)),
                whole((rows, units)),
                whole((rows, 2 * units)),
            ],
            scratch_shapes=[
                pltpu.VMEM((rows, 2 * units), F32),
                pltpu.VMEM((rows, units), F32),
                pltpu.VMEM((main, block), F32),
                pltpu.VMEM((rows, 1), F32),
            ],
        ),
        out_shape=[
            shape_of((rows, width)),
            shape_of((rows, width)),
            shape_of((main, width + block + LANES)),
            shape_of((rows, units)),
            shape_of((rows, 2 * units)),
        ],
        compiler_params=params(),
        cost_estimate=costs(16),
    )(coords, slices, *gates, *ups, *downs)


def combine_kernel(
    left,
    coords_ref,
    main_ref,
    folded_ref,
    probe_ref,
    places_ref,
    dense_own_ref,
    dense_other_ref,
    total_ref,
):
    step = pl.program_id(0)
    quarters = pl.num_programs(0)
    quarter = lax.rem(coords_ref[1] * (quarters // 2) + step, quarters)
    slots = main_ref.shape[0]
    parts, tall, tokens = total_ref.shape
    feats = tall - TILE
    lane = lax.broadcasted_iota(jnp.int32, (tokens, slots), 1)
    down = (((0,), (1,)), ((), ()))
    pick = lambda place: jnp.where(lane == place, 1.0, 0.0).astype(BF16)
    first = [pick(places_ref[:, k : k + 1]) for k in range(TOP)]
    shifted = [pick(places_ref[:, TOP + k : TOP + k + 1] + quarter * left) for k in range(TOP)]
    rows = lax.dot_general(
        main_ref[...], first[0] + first[1], down, preferred_element_type=F32
    ) + lax.dot_general(
        folded_ref[...], shifted[0] + shifted[1], down, preferred_element_type=F32
    )
    dense = jnp.where(step < quarters // 2, dense_own_ref[...], dense_other_ref[...])
    rows = (dense + rows).astype(BF16)
    for part in range(parts):
        total_ref[part, :feats, :] = rows[part * feats : (part + 1) * feats]
    probes = []
    for k in range(TOP):
        near = lax.dot_general(probe_ref[...], first[k], down, preferred_element_type=F32)
        far = pick(places_ref[:, TOP + k : TOP + k + 1])
        far = lax.dot_general(probe_ref[...], far, down, preferred_element_type=F32)
        probes.append(near[0:1] + near[1:2] + (far[2:3] + far[3:4]))
    probes = jnp.concatenate(probes, axis=0)
    high = probes.astype(BF16).astype(F32)
    empty = jnp.zeros((TILE - 2 * TOP, tokens), F32)
    extra = jnp.concatenate([high, probes - high, empty], axis=0).astype(BF16)
    for part in range(parts):
        total_ref[part, feats:, :] = extra


def combine(back, coords, places, dense_own, dense_other, size, capacity):
    half_width, tokens = dense_own.shape
    width = 2 * half_width
    left = capacity - TILE
    quarters = TILE // left
    block = width // quarters
    slots = back.shape[0]
    feats = width // size
    last = quarters // 2 - 1
    return pl.pallas_call(
        functools.partial(combine_kernel, left),
        grid_spec=pltpu.PrefetchScalarGridSpec(
            num_scalar_prefetch=1,
            grid=(quarters,),
            in_specs=[
                pl.BlockSpec(
                    (slots, block), lambda i, c: (0, lax.rem(c[1] * (quarters // 2) + i, quarters))
                ),
                pl.BlockSpec((slots, block), lambda i, c: (0, quarters)),
                pl.BlockSpec((slots, LANES), lambda i, c: (0, (quarters + 1) * block // LANES)),
                pl.BlockSpec((tokens, 2 * TOP), lambda i, c: (0, 0)),
                pl.BlockSpec((block, tokens), lambda i, c: (jnp.minimum(i, last), 0)),
                pl.BlockSpec((block, tokens), lambda i, c: (jnp.maximum(i, last + 1) - last - 1, 0)),
            ],
            out_specs=pl.BlockSpec(
                (size // quarters, feats + TILE, tokens),
                lambda i, c: (lax.rem(c[1] * (quarters // 2) + i, quarters), 0, 0),
            ),
        ),
        out_shape=jax.ShapeDtypeStruct((size, feats + TILE, tokens), BF16),
        compiler_params=pltpu.CompilerParams(
            dimension_semantics=("arbitrary",), vmem_limit_bytes=VMEM_LIMIT
        ),
        cost_estimate=costs(6),
    )(coords, back, back, back, places, dense_own, dense_other)


def local(
    layer_input,
    cotangent,
    route_probs,
    routes,
    shared_gate,
    shared_up,
    shared_down,
    routed_gate,
    routed_up,
    routed_down,
):
    tok_rows, feats = layer_input.shape
    experts = lax.axis_size("expert")
    capacity = 5 * TOP * tok_rows // (4 * experts)

    both = jnp.concatenate([layer_input.T, cotangent.T], axis=0)
    coords = jnp.stack([lax.axis_index("tensor"), lax.axis_index("dp")]).astype(jnp.int32)

    def with_other(own):
        return own, swap(own)

    dense_weights = [
        with_other(weight) for weight in (shared_gate.T, shared_up.T, shared_down)
    ]
    expert_weights = [
        with_other(weight) for weight in (routed_gate[0].T, routed_up[0].T, routed_down[0])
    ]

    folded, places = dispatch(routes.T, route_probs.T, both, experts, capacity)
    size = lax.axis_size("tensor")
    arrived = lax.all_to_all(
        folded.reshape(experts, TILE, -1), "expert", split_axis=0, concat_axis=0, tiled=True
    )
    pieces = single_ring(both, range(1, size // 2 + 1))[0] + [(both, 0)]
    distances = [piece[1] for piece in pieces]
    arrived, pieces, dense_weights = lax.optimization_barrier(
        (arrived, [piece[0] for piece in pieces], dense_weights)
    )
    pieces = list(zip(pieces, distances))
    slices = lax.all_gather(
        arrived.reshape(experts * TILE, -1), "tensor", axis=0, tiled=False
    )

    own_rows, dense_backs, dense_hidden, pair_terms, down_terms = dense_forward(
        pieces, coords, *dense_weights
    )
    terms = dense_terms(own_rows, dense_backs, dense_hidden, swap(pair_terms), swap(down_terms))
    terms = terms.reshape(experts, -1, terms.shape[1])
    terms = lax.all_to_all(terms, "expert", split_axis=0, concat_axis=0, tiled=True)
    units = dense_hidden.shape[0]
    dense_own, dense_other = [
        product("hd,hn->dn", gate, dense_backs[:units])
        + product("hd,hn->dn", up, dense_backs[units:])
        for gate, up in zip(*dense_weights[:2])
    ]

    slot_in, scaled_out, sent, hidden, backs = expert_rows(
        slices, coords, *expert_weights, experts, capacity
    )
    sent, terms = lax.optimization_barrier((sent, terms))
    terms = terms.astype(F32).sum(axis=0).astype(BF16)
    first = lane_up(2 * units)
    grad_gate = terms[:, :units]
    grad_up = terms[:, units : 2 * units]
    grad_down = terms[:, first : first + units].T
    back = lax.all_to_all(
        sent.reshape(experts, TILE, -1), "expert", split_axis=0, concat_axis=0, tiled=True
    )

    def reduced(rows, backs):
        own, other = halves(rows, 1)
        arrived = swap(product("sh,sd->hd", backs, other).astype(BF16))
        return (product("sh,sd->hd", backs, own) + arrived.astype(F32)).astype(BF16)

    delta_pair = reduced(slot_in, backs)
    delta_gate = delta_pair[:units].T[None]
    delta_up = delta_pair[units:].T[None]
    delta_down = reduced(scaled_out, hidden)[None]

    total = combine(
        back.reshape(experts * TILE, -1),
        coords,
        places,
        dense_own,
        dense_other,
        lax.axis_size("tensor"),
        capacity,
    )
    total = lax.all_to_all(total, "tensor", split_axis=0, concat_axis=0, tiled=True)
    total = total.astype(F32).sum(axis=0)
    input_grad = total[:feats].T.astype(BF16)
    prob_grad = (total[feats : feats + TOP] + total[feats + TOP : feats + 2 * TOP]).T
    return (
        input_grad,
        prob_grad,
        grad_gate,
        grad_up,
        grad_down,
        delta_gate,
        delta_up,
        delta_down,
    )


def solution(mesh):
    return jax.shard_map(
        local,
        mesh=mesh,
        in_specs=(
            P(("dp", "expert"), "tensor"),
            P(("dp", "expert"), "tensor"),
            P(("dp", "expert"), None),
            P(("dp", "expert"), None),
            P("dp", "tensor"),
            P("dp", "tensor"),
            P("tensor", "dp"),
            P("expert", "dp", "tensor"),
            P("expert", "dp", "tensor"),
            P("expert", "tensor", "dp"),
        ),
        out_specs=(
            P(("dp", "expert"), "tensor"),
            P(("dp", "expert"), None),
            P(("dp", "expert"), "tensor"),
            P(("dp", "expert"), "tensor"),
            P("tensor", ("dp", "expert")),
            P("expert", "dp", "tensor"),
            P("expert", "dp", "tensor"),
            P("expert", "tensor", "dp"),
        ),
        check_vma=False,
    )
```

profile of v0, /device:TPU:19, one launch (start us, length us, event | category | flops | bytes accessed | tf_op | source)
XLA Modules:
  0.0 223.7 jit_solution(10698402457709625658)
XLA Ops:
  7.2 0.8 collective-permute-start.7
  7.9 0.1 collective-permute-start.8
  8.0 0.4 collective-permute-start.9
  8.4 1.0 pad_maximum_fusion.both_ref.refs_7_
  9.4 1.7 collective-permute-start
  11.2 4.0 %collective-permute-start.1 = (bf16[896,128]{1,0:T(8,128)(2,1)S(1)}, bf16[896,128]{1,0:T(8,128)(2,1)S(1)}, u32[]{:S(2)}, u32[]{:S(2)}) collective-permute-start(bf16[896,128]{1,0:T(8,128)(2,1)S(1)} %pad_maximum_fusion.both_ref.refs_7_), channel_id=1, source_target_pairs={{0,7},{1,0},{2,1},{3,2},{4,3},{5,4},{6,5},{7,6},{8,15},{9,8},{10,9... | collective-permute-start | bytes 688136 | tf_op jit(solution)/shard_map/ppermute | solution.py:28
  15.2 5.8 %collective-permute-done.refs_0_ = bf16[896,128]{1,0:T(8,128)(2,1)S(1)} collective-permute-done((bf16[896,128]{1,0:T(8,128)(2,1)S(1)}, bf16[896,128]{1,0:T(8,128)(2,1)S(1)}, u32[]{:S(2)}, u32[]{:S(2)}) %collective-permute-start) | collective-permute-done | bytes 229408 | tf_op jit(solution)/shard_map/ppermute | solution.py:28
  21.0 2.9 %shard_map.161 = (bf16[256,1152]{1,0:T(8,128)(2,1)}, s32[128,4]{1,0:T(8,128)}) custom-call(s32[2,128]{1,0:T(2,128)} %bitcast.65, f32[2,128]{1,0:T(2,128)} %bitcast.66, bf16[896,128]{1,0:T(8,128)(2,1)} %copy-done.9), custom_call_target="tpu_custom_call" | custom-call | flops 1 | bytes 10500000 | tf_op jit(solution)/shard_map/pallas_call | solution.py:134
  23.9 6.7 %all-to-all-start = ((bf16[16,16,1152]{2,1,0:T(8,128)(2,1)}), bf16[16,16,1152]{2,1,0:T(8,128)(2,1)S(1)}, u32[]{:S(2)}, u32[]{:S(2)}) async-start(bf16[16,16,1152]{2,1,0:T(8,128)(2,1)} %bitcast.62), calls=%async_computation | async-start | bytes 1179648 | tf_op jit(solution)/shard_map/all_to_all | solution.py:612
  30.6 0.0 all-gather.2.cloned.1.call-start
  30.7 2.7 %collective-permute-start.3 = (bf16[896,128]{1,0:T(8,128)(2,1)S(1)}, bf16[896,128]{1,0:T(8,128)(2,1)S(1)}, u32[]{:S(2)}, u32[]{:S(2)}) collective-permute-start(bf16[896,128]{1,0:T(8,128)(2,1)S(1)} %collective-permute-done.1.refs_1_), channel_id=1, source_target_pairs={{0,7},{1,0},{2,1},{3,2},{4,3},{5,4},{6,5},{7,6},{8,15},{9,8},{10,9... | collective-permute-start | bytes 688136 | tf_op jit(solution)/shard_map/ppermute | solution.py:28
  33.3 3.4 %collective-permute-done.3.refs_3_ = bf16[896,128]{1,0:T(8,128)(2,1)S(1)} collective-permute-done((bf16[896,128]{1,0:T(8,128)(2,1)S(1)}, bf16[896,128]{1,0:T(8,128)(2,1)S(1)}, u32[]{:S(2)}, u32[]{:S(2)}) %collective-permute-start.3) | collective-permute-done | bytes 229408 | tf_op jit(solution)/shard_map/ppermute | solution.py:28
  36.7 3.4 %collective-permute-start.5 = (bf16[896,128]{1,0:T(8,128)(2,1)S(1)}, bf16[896,128]{1,0:T(8,128)(2,1)}, u32[]{:S(2)}, u32[]{:S(2)}) collective-permute-start(bf16[896,128]{1,0:T(8,128)(2,1)S(1)} %collective-permute-done.3.refs_3_), channel_id=1, source_target_pairs={{0,7},{1,0},{2,1},{3,2},{4,3},{5,4},{6,5},{7,6},{8,15},{9,8},{10,9... | collective-permute-start | bytes 688136 | tf_op jit(solution)/shard_map/ppermute | solution.py:28
  40.1 0.0 collective-permute-done.4.refs_4_
  40.2 2.9 %collective-permute-done.5.refs_5_ = bf16[896,128]{1,0:T(8,128)(2,1)} collective-permute-done((bf16[896,128]{1,0:T(8,128)(2,1)S(1)}, bf16[896,128]{1,0:T(8,128)(2,1)}, u32[]{:S(2)}, u32[]{:S(2)}) %collective-permute-start.5) | collective-permute-done | bytes 229408 | tf_op jit(solution)/shard_map/ppermute | solution.py:28
  43.1 3.5 %collective-permute-done.6.refs_6_ = bf16[896,128]{1,0:T(8,128)(2,1)} collective-permute-done((bf16[896,128]{1,0:T(8,128)(2,1)}, bf16[896,128]{1,0:T(8,128)(2,1)}, u32[]{:S(2)}, u32[]{:S(2)}) %collective-permute-start.6) | collective-permute-done | bytes 229408 | tf_op jit(solution)/shard_map/ppermute | solution.py:28
  46.6 0.0 all-gather.2.cloned.1.call-update
  46.6 0.7 pad_add_fusion.coords_ref
  47.3 0.2 copy-done.2
  47.5 0.4 copy-done.5
  47.9 11.0 %shard_map.163 = (bf16[4,896,128]{2,1,0:T(8,128)(2,1)}, bf16[608,128]{1,0:T(8,128)(2,1)}, bf16[304,128]{1,0:T(8,128)(2,1)}, bf16[1792,640]{1,0:T(8,128)(2,1)}, bf16[1792,384]{1,0:T(8,128)(2,1)}) custom-call(s32[2]{0:T(128)} %pad_add_fusion.coords_ref, bf16[896,128]{1,0:T(8,128)(2,1)} %copy-done.17, bf16[896,128]{1,0:T(8,128)(2,1)} %copy-done.18, ...), custom_call_target="tpu_custom_call" | custom-call | flops 1 | bytes 35000000 | tf_op jit(solution)/shard_map/pallas_call | solution.py:239
  58.9 4.0 %collective-permute-start.13 = (bf16[1792,640]{1,0:T(8,128)(2,1)}, bf16[1792,640]{1,0:T(8,128)(2,1)S(1)}, u32[]{:S(2)}, u32[]{:S(2)}) collective-permute-start(bf16[1792,640]{1,0:T(8,128)(2,1)} %get-tuple-element.57), channel_id=1, source_target_pairs={{0,128},{128,0},{1,129},{129,1},{2,130},{130,2},{3,131},{131,3},{4... | collective-permute-start | bytes 6881288 | tf_op jit(solution)/shard_map/ppermute | solution.py:23
  62.9 0.1 collective-permute-start.14
  63.0 6.1 %collective-permute-done.14.down_arrived_ref = bf16[1792,384]{1,0:T(8,128)(2,1)S(1)} collective-permute-done((bf16[1792,384]{1,0:T(8,128)(2,1)}, bf16[1792,384]{1,0:T(8,128)(2,1)S(1)}, u32[]{:S(2)}, u32[]{:S(2)}) %collective-permute-start.14) | collective-permute-done | bytes 1376288 | tf_op jit(solution)/shard_map/ppermute | solution.py:23
  69.2 1.2 copy-done.11
  70.4 0.7 copy-done.8
  71.0 4.6 %shard_map.164 = bf16[1792,1024]{1,0:T(8,128)(2,1)} custom-call(bf16[4,896,128]{2,1,0:T(8,128)(2,1)} %get-tuple-element.54.both_ref, bf16[608,128]{1,0:T(8,128)(2,1)} %get-tuple-element.55.backs_ref, bf16[304,128]{1,0:T(8,128)(2,1)} %get-tuple-element.56.hidden_ref, bf16[1792,640]{1,0:T(8,128)(2,1)} %copy-done.8, bf16[1792,384]{1,0:T(8,128)(2,1)} %copy-done.11), custom_call_target="tpu_custom_call" | custom-call | flops 1 | bytes 17500000 | tf_op jit(solution)/shard_map/pallas_call | solution.py:297
  75.6 7.1 %all-to-all-start.1 = ((bf16[16,112,1024]{2,1,0:T(8,128)(2,1)}), bf16[16,112,1024]{2,1,0:T(8,128)(2,1)}, u32[]{:S(2)}, u32[]{:S(2)}) async-start(bf16[16,112,1024]{2,1,0:T(8,128)(2,1)} %bitcast.47), calls=%async_computation.1 | async-start | bytes 7340032 | tf_op jit(solution)/shard_map/all_to_all | solution.py:630
  82.8 1.0 collective-permute-start.10
  83.8 0.1 collective-permute-start.11
  83.9 0.4 collective-permute-start.12
  84.3 1.8 collective-permute-done.10.gate_other_ref
  86.1 3.1 %collective-permute-done.11.up_other_ref = bf16[304,1792]{1,0:T(8,128)(2,1)S(1)} collective-permute-done((bf16[304,1792]{1,0:T(8,128)(2,1)S(1)}, bf16[304,1792]{1,0:T(8,128)(2,1)S(1)}, u32[]{:S(2)}, u32[]{:S(2)}) %collective-permute-start.11) | collective-permute-done | bytes 1089568 | tf_op jit(solution)/shard_map/ppermute | solution.py:23
  89.2 1.0 copy-done.16
  90.2 19.2 %all-gather.2.cloned.1.call-done.slices_ref = bf16[8,256,1152]{2,1,0:T(8,128)(2,1)} async-done(((bf16[1,256,1152]{2,1,0:T(8,128)(2,1)}), bf16[8,256,1152]{2,1,0:T(8,128)(2,1)}) %all-gather.2.cloned.1.call-update) | async-done | bytes 4718608 | tf_op jit(solution)/shard_map/all_gather | solution.py:621
  109.4 17.0 %shard_map.162 = (bf16[320,3584]{1,0:T(8,128)(2,1)}, bf16[320,3584]{1,0:T(8,128)(2,1)}, bf16[256,4608]{1,0:T(8,128)(2,1)}, bf16[320,304]{1,0:T(8,128)(2,1)}, bf16[320,608]{1,0:T(8,128)(2,1)}) custom-call(s32[2]{0:T(128)} %pad_add_fusion.coords_ref, bf16[8,256,1152]{2,1,0:T(8,128)(2,1)} %all-gather.2.cloned.1.call-done.slices_ref, ...), custom_call_target="tpu_custom_call" | custom-call | flops 1 | bytes 56000000 | tf_op jit(solution)/shard_map/pallas_call | solution.py:465
  126.4 2.9 %all-to-all-done.1 = bf16[16,112,1024]{2,1,0:T(8,128)(2,1)} async-done(((bf16[16,112,1024]{2,1,0:T(8,128)(2,1)}), bf16[16,112,1024]{2,1,0:T(8,128)(2,1)}, u32[]{:S(2)}, u32[]{:S(2)}) %all-to-all-start.1) | async-done | bytes 3670048 | tf_op jit(solution)/shard_map/all_to_all | solution.py:630
  129.3 16.7 %all-to-all-start.2 = ((bf16[16,16,4608]{2,1,0:T(8,128)(2,1)}), bf16[16,16,4608]{2,1,0:T(8,128)(2,1)S(1)}, u32[]{:S(2)}, u32[]{:S(2)}) async-start(bf16[16,16,4608]{2,1,0:T(8,128)(2,1)} %bitcast.54), calls=%async_computation.2 | async-start | bytes 4718592 | tf_op jit(solution)/shard_map/all_to_all | solution.py:647
  146.0 4.0 %convolution_convert_fusion = bf16[608,1792]{1,0:T(8,128)(2,1)} fusion(bf16[320,608]{1,0:T(8,128)(2,1)S(1)} %copy-done.22, bf16[320,3584]{1,0:T(8,128)(2,1)} %get-tuple-element.63, s32[]{:T(128)S(6)} %select_n.9), kind=kOutput, calls=%fused_computation.1 | convolution fusion | flops 698392576 | bytes 3715076 | tf_op jit(solution)/shard_map/sh,sd->hd/dot_general | solution.py:19
  150.1 2.1 collective-permute-start.15
  152.2 0.6 fusion.7
  152.8 1.5 convolution_add_fusion.1.dense_other_ref
  154.3 0.2 copy-done.21
  154.5 0.2 copy-done.24
  154.7 1.7 convolution_convert_fusion.1
  156.5 0.6 collective-permute-start.16
  157.1 0.6 fusion.9
  157.7 1.5 convolution_add_fusion.2.dense_own_ref
  159.2 15.6 %all-to-all-done.2 = bf16[16,16,4608]{2,1,0:T(8,128)(2,1)S(1)} async-done(((bf16[16,16,4608]{2,1,0:T(8,128)(2,1)}), bf16[16,16,4608]{2,1,0:T(8,128)(2,1)S(1)}, u32[]{:S(2)}, u32[]{:S(2)}) %all-to-all-start.2) | async-done | bytes 2359328 | tf_op jit(solution)/shard_map/all_to_all | solution.py:647
  174.9 1.4 copy-done
  176.3 6.2 %shard_map.165 = bf16[8,464,128]{2,1,0:T(8,128)(2,1)} custom-call(s32[2]{0:T(128)} %pad_add_fusion.coords_ref, bf16[256,4608]{1,0:T(8,128)(2,1)} %bitcast.44, bf16[256,4608]{1,0:T(8,128)(2,1)} %bitcast.45, bf16[256,4608]{1,0:T(8,128)(2,1)} %bitcast.46, s32[128,4]{1,0:T(8,128)} %get-tuple-element.60.places_ref, ...), custom_call_target="tpu_custom_call" | custom-call | flops 1 | bytes 21000000 | tf_op jit(solution)/shard_map/pallas_call | solution.py:553
  182.5 5.8 %all-to-all-start.3 = ((bf16[8,464,128]{2,1,0:T(8,128)(2,1)}), bf16[8,464,128]{2,1,0:T(8,128)(2,1)S(1)}, u32[]{:S(2)}, u32[]{:S(2)}) async-start(bf16[8,464,128]{2,1,0:T(8,128)(2,1)} %shard_map.165), calls=%async_computation.3 | async-start | bytes 1900544 | tf_op jit(solution)/shard_map/all_to_all | solution.py:670
  188.4 2.9 %reduce_sum.22 = bf16[112,1024]{1,0:T(8,128)(2,1)S(1)} reduce(bf16[16,112,1024]{2,1,0:T(8,128)(2,1)} %all-to-all-done.1, bf16[]{:T(256)} %constant.6.clone.1), dimensions={0}, to_apply=%region_1.0 | reduce | flops 1720320 | bytes 3899394 | tf_op jit(solution)/shard_map/reduce_sum | solution.py:642
  191.3 0.1 slice_bitcast_fusion.2
  191.4 0.7 copy.18
  192.1 0.7 copy.19
  192.8 0.7 copy.20
  193.6 3.2 %fusion.1 = bf16[1,304,1792]{2,1,0:T(8,128)(2,1)} fusion(bf16[320,304]{1,0:T(8,128)(2,1)S(1)} %copy-done.25, bf16[304,1792]{1,0:T(8,128)(2,1)S(1)} %collective-permute-done.16, bf16[320,3584]{1,0:T(8,128)(2,1)} %get-tuple-element.65, s32[]{:T(128)S(6)} %select_n.8), kind=kOutput, calls=%fused_computation.5 | convolution fusion | flops 350285824 | bytes 3520516 | tf_op jit(solution)/shard_map/sh,sd->hd/dot_general | solution.py:19
  196.8 3.0 %add_convert_fusion = bf16[608,1792]{1,0:T(8,128)(2,1)S(1)} fusion(bf16[608,1792]{1,0:T(8,128)(2,1)} %collective-permute-done.15, bf16[320,608]{1,0:T(8,128)(2,1)S(1)} %copy-done.23, bf16[320,3584]{1,0:T(8,128)(2,1)S(1)} %copy-done.20, s32[]{:T(128)S(6)} %select_n.8), kind=kOutput, calls=%fused_computation | convolution fusion | flops 700571648 | bytes 5914628 | tf_op jit(solution)/shard_map/sh,sd->hd/dot_general | solution.py:19
  199.7 1.5 slice_bitcast_fusion
  201.2 14.2 %all-to-all-done.3 = bf16[8,464,128]{2,1,0:T(8,128)(2,1)S(1)} async-done(((bf16[8,464,128]{2,1,0:T(8,128)(2,1)}), bf16[8,464,128]{2,1,0:T(8,128)(2,1)S(1)}, u32[]{:S(2)}, u32[]{:S(2)}) %all-to-all-start.3) | async-done | bytes 950304 | tf_op jit(solution)/shard_map/all_to_all | solution.py:670
  215.5 0.1 convert_reduce_fusion
  215.6 0.7 fusion.6
  216.3 0.6 fusion.13
  (57 shorter events, 0.1 us)
Async XLA Ops:
  7.2 39.4 %collective-permute-start.7 = (bf16[304,1792]{1,0:T(8,128)(2,1)}, bf16[304,1792]{1,0:T(8,128)(2,1)S(1)}, u32[]{:S(2)}, u32[]{:S(2)}) collective-permute-start(bf16[304,1792]{1,0:T(8,128)(2,1)} %bitcast.48), channel_id=1, source_target_pairs={{0,128},{128,0},{1,129},{129,1},{2,130},{130,2},{3,131},{131,3},{4... | collective-permute-start | bytes 3268616 | tf_op jit(solution)/shard_map/ppermute | solution.py:23
  7.9 38.6 %collective-permute-start.8 = (bf16[304,1792]{1,0:T(8,128)(2,1)}, bf16[304,1792]{1,0:T(8,128)(2,1)S(1)}, u32[]{:S(2)}, u32[]{:S(2)}) collective-permute-start(bf16[304,1792]{1,0:T(8,128)(2,1)} %bitcast.51), channel_id=1, source_target_pairs={{0,128},{128,0},{1,129},{129,1},{2,130},{130,2},{3,131},{131,3},{4... | collective-permute-start | bytes 3268616 | tf_op jit(solution)/shard_map/ppermute | solution.py:23
  8.0 38.5 %collective-permute-start.9 = (bf16[304,1792]{1,0:T(8,128)(2,1)}, bf16[304,1792]{1,0:T(8,128)(2,1)}, u32[]{:S(2)}, u32[]{:S(2)}) collective-permute-start(bf16[304,1792]{1,0:T(8,128)(2,1)} %refs_12_), channel_id=1, source_target_pairs={{0,128},{128,0},{1,129},{129,1},{2,130},{130,2},{3,131},{131,3},{4... | collective-permute-start | bytes 3268616 | tf_op jit(solution)/shard_map/ppermute | solution.py:23
  9.4 11.6 %copy-start.9 = (bf16[896,128]{1,0:T(8,128)(2,1)}, bf16[896,128]{1,0:T(8,128)(2,1)S(1)}, u32[]{:S(2)}) copy-start(bf16[896,128]{1,0:T(8,128)(2,1)S(1)} %pad_maximum_fusion.both_ref.refs_7_) | copy-start | bytes 688132
  9.4 11.5 %collective-permute-start = (bf16[896,128]{1,0:T(8,128)(2,1)S(1)}, bf16[896,128]{1,0:T(8,128)(2,1)S(1)}, u32[]{:S(2)}, u32[]{:S(2)}) collective-permute-start(bf16[896,128]{1,0:T(8,128)(2,1)S(1)} %pad_maximum_fusion.both_ref.refs_7_), channel_id=1, source_target_pairs={{0,1},{1,2},{2,3},{3,4},{4,5},{5,6},{6,7},{7,0},{8,9},{9,10},{10,1... | collective-permute-start | bytes 688136 | tf_op jit(solution)/shard_map/ppermute | solution.py:28
  11.2 19.5 %collective-permute-start.1 = (bf16[896,128]{1,0:T(8,128)(2,1)S(1)}, bf16[896,128]{1,0:T(8,128)(2,1)S(1)}, u32[]{:S(2)}, u32[]{:S(2)}) collective-permute-start(bf16[896,128]{1,0:T(8,128)(2,1)S(1)} %pad_maximum_fusion.both_ref.refs_7_), channel_id=1, source_target_pairs={{0,7},{1,0},{2,1},{3,2},{4,3},{5,4},{6,5},{7,6},{8,15},{9,8},{10,9... | collective-permute-start | bytes 688136 | tf_op jit(solution)/shard_map/ppermute | solution.py:28
  21.0 26.4 %copy-start.17 = (bf16[896,128]{1,0:T(8,128)(2,1)}, bf16[896,128]{1,0:T(8,128)(2,1)S(1)}, u32[]{:S(2)}) copy-start(bf16[896,128]{1,0:T(8,128)(2,1)S(1)} %collective-permute-done.refs_0_) | copy-start | bytes 688132
  21.0 12.4 %collective-permute-start.2 = (bf16[896,128]{1,0:T(8,128)(2,1)S(1)}, bf16[896,128]{1,0:T(8,128)(2,1)}, u32[]{:S(2)}, u32[]{:S(2)}) collective-permute-start(bf16[896,128]{1,0:T(8,128)(2,1)S(1)} %collective-permute-done.refs_0_), channel_id=1, source_target_pairs={{0,1},{1,2},{2,3},{3,4},{4,5},{5,6},{6,7},{7,0},{8,9},{9,10},{10,1... | collective-permute-start | bytes 688136 | tf_op jit(solution)/shard_map/ppermute | solution.py:28
  23.9 16.3 %all-to-all-start = ((bf16[16,16,1152]{2,1,0:T(8,128)(2,1)}), bf16[16,16,1152]{2,1,0:T(8,128)(2,1)S(1)}, u32[]{:S(2)}, u32[]{:S(2)}) async-start(bf16[16,16,1152]{2,1,0:T(8,128)(2,1)} %bitcast.62), calls=%async_computation | async-start | bytes 1179648 | tf_op jit(solution)/shard_map/all_to_all | solution.py:612
  30.6 78.8 %all-gather.2.cloned.1.call-start = ((), (), s32[]{:S(2)}) async-start(), calls=%async_computation.4 | async-start | bytes 5308416 | tf_op jit(solution)/shard_map/all_gather | solution.py:621
  30.7 16.7 %copy-start.18 = (bf16[896,128]{1,0:T(8,128)(2,1)}, bf16[896,128]{1,0:T(8,128)(2,1)S(1)}, u32[]{:S(2)}) copy-start(bf16[896,128]{1,0:T(8,128)(2,1)S(1)} %collective-permute-done.1.refs_1_) | copy-start | bytes 688132
  30.7 6.0 %collective-permute-start.3 = (bf16[896,128]{1,0:T(8,128)(2,1)S(1)}, bf16[896,128]{1,0:T(8,128)(2,1)S(1)}, u32[]{:S(2)}, u32[]{:S(2)}) collective-permute-start(bf16[896,128]{1,0:T(8,128)(2,1)S(1)} %collective-permute-done.1.refs_1_), channel_id=1, source_target_pairs={{0,7},{1,0},{2,1},{3,2},{4,3},{5,4},{6,5},{7,6},{8,15},{9,8},{10,9... | collective-permute-start | bytes 688136 | tf_op jit(solution)/shard_map/ppermute | solution.py:28
  33.3 6.8 %collective-permute-start.4 = (bf16[896,128]{1,0:T(8,128)(2,1)}, bf16[896,128]{1,0:T(8,128)(2,1)}, u32[]{:S(2)}, u32[]{:S(2)}) collective-permute-start(bf16[896,128]{1,0:T(8,128)(2,1)} %collective-permute-done.2.refs_2_), channel_id=1, source_target_pairs={{0,1},{1,2},{2,3},{3,4},{4,5},{5,6},{6,7},{7,0},{8,9},{9,10},{10,1... | collective-permute-start | bytes 688136 | tf_op jit(solution)/shard_map/ppermute | solution.py:28
  36.7 10.6 %copy-start.19 = (bf16[896,128]{1,0:T(8,128)(2,1)}, bf16[896,128]{1,0:T(8,128)(2,1)S(1)}, u32[]{:S(2)}) copy-start(bf16[896,128]{1,0:T(8,128)(2,1)S(1)} %collective-permute-done.3.refs_3_) | copy-start | bytes 688132
  36.7 6.4 %collective-permute-start.5 = (bf16[896,128]{1,0:T(8,128)(2,1)S(1)}, bf16[896,128]{1,0:T(8,128)(2,1)}, u32[]{:S(2)}, u32[]{:S(2)}) collective-permute-start(bf16[896,128]{1,0:T(8,128)(2,1)S(1)} %collective-permute-done.3.refs_3_), channel_id=1, source_target_pairs={{0,7},{1,0},{2,1},{3,2},{4,3},{5,4},{6,5},{7,6},{8,15},{9,8},{10,9... | collective-permute-start | bytes 688136 | tf_op jit(solution)/shard_map/ppermute | solution.py:28
  40.2 6.4 %collective-permute-start.6 = (bf16[896,128]{1,0:T(8,128)(2,1)}, bf16[896,128]{1,0:T(8,128)(2,1)}, u32[]{:S(2)}, u32[]{:S(2)}) collective-permute-start(bf16[896,128]{1,0:T(8,128)(2,1)} %collective-permute-done.4.refs_4_), channel_id=1, source_target_pairs={{0,1},{1,2},{2,3},{3,4},{4,5},{5,6},{6,7},{7,0},{8,9},{9,10},{10,1... | collective-permute-start | bytes 688136 | tf_op jit(solution)/shard_map/ppermute | solution.py:28
  40.2 6.4 %copy-start.7 = (bf16[16,16,1152]{2,1,0:T(8,128)(2,1)}, bf16[16,16,1152]{2,1,0:T(8,128)(2,1)S(1)}, u32[]{:S(2)}) copy-start(bf16[16,16,1152]{2,1,0:T(8,128)(2,1)S(1)} %all-to-all-done) | copy-start | bytes 1769476
  46.6 1.0 copy-start.2
  46.6 1.3 copy-start.5
  58.9 10.3 %collective-permute-start.13 = (bf16[1792,640]{1,0:T(8,128)(2,1)}, bf16[1792,640]{1,0:T(8,128)(2,1)S(1)}, u32[]{:S(2)}, u32[]{:S(2)}) collective-permute-start(bf16[1792,640]{1,0:T(8,128)(2,1)} %get-tuple-element.57), channel_id=1, source_target_pairs={{0,128},{128,0},{1,129},{129,1},{2,130},{130,2},{3,131},{131,3},{4... | collective-permute-start | bytes 6881288 | tf_op jit(solution)/shard_map/ppermute | solution.py:23
  62.9 6.2 %collective-permute-start.14 = (bf16[1792,384]{1,0:T(8,128)(2,1)}, bf16[1792,384]{1,0:T(8,128)(2,1)S(1)}, u32[]{:S(2)}, u32[]{:S(2)}) collective-permute-start(bf16[1792,384]{1,0:T(8,128)(2,1)} %get-tuple-element.58), channel_id=1, source_target_pairs={{0,128},{128,0},{1,129},{129,1},{2,130},{130,2},{3,131},{131,3},{4... | collective-permute-start | bytes 4128776 | tf_op jit(solution)/shard_map/ppermute | solution.py:23
  69.2 1.2 copy-start.11
  69.2 1.8 copy-start.8
  75.6 7.1 %copy-start.12 = (bf16[1,1792,304]{1,2,0:T(8,128)(2,1)S(1)}, bf16[1,1792,304]{1,2,0:T(8,128)(2,1)}, u32[]{:S(2)}) copy-start(bf16[1,1792,304]{1,2,0:T(8,128)(2,1)} %param.17) | copy-start | bytes 3268612
  75.6 8.1 %copy-start.13 = (bf16[1,1792,304]{1,2,0:T(8,128)(2,1)S(1)}, bf16[1,1792,304]{1,2,0:T(8,128)(2,1)}, u32[]{:S(2)}) copy-start(bf16[1,1792,304]{1,2,0:T(8,128)(2,1)} %param.18) | copy-start | bytes 3268612
  75.6 8.2 %copy-start.14 = (bf16[1,304,1792]{2,1,0:T(8,128)(2,1)S(1)}, bf16[1,304,1792]{2,1,0:T(8,128)(2,1)}, u32[]{:S(2)}) copy-start(bf16[1,304,1792]{2,1,0:T(8,128)(2,1)} %param.19) | copy-start | bytes 3268612
  75.6 53.7 %all-to-all-start.1 = ((bf16[16,112,1024]{2,1,0:T(8,128)(2,1)}), bf16[16,112,1024]{2,1,0:T(8,128)(2,1)}, u32[]{:S(2)}, u32[]{:S(2)}) async-start(bf16[16,112,1024]{2,1,0:T(8,128)(2,1)} %bitcast.47), calls=%async_computation.1 | async-start | bytes 7340032 | tf_op jit(solution)/shard_map/all_to_all | solution.py:630
  82.8 3.3 %collective-permute-start.10 = (bf16[304,1792]{1,0:T(8,128)(2,1)S(1)}, bf16[304,1792]{1,0:T(8,128)(2,1)S(1)}, u32[]{:S(2)}, u32[]{:S(2)}) collective-permute-start(bf16[304,1792]{1,0:T(8,128)(2,1)S(1)} %bitcast.57), channel_id=1, source_target_pairs={{0,128},{128,0},{1,129},{129,1},{2,130},{130,2},{3,131},{131,3},{4... | collective-permute-start | bytes 3268616 | tf_op jit(solution)/shard_map/ppermute | solution.py:23
  83.8 5.5 %collective-permute-start.11 = (bf16[304,1792]{1,0:T(8,128)(2,1)S(1)}, bf16[304,1792]{1,0:T(8,128)(2,1)S(1)}, u32[]{:S(2)}, u32[]{:S(2)}) collective-permute-start(bf16[304,1792]{1,0:T(8,128)(2,1)S(1)} %bitcast.59), channel_id=1, source_target_pairs={{0,128},{128,0},{1,129},{129,1},{2,130},{130,2},{3,131},{131,3},{4... | collective-permute-start | bytes 3268616 | tf_op jit(solution)/shard_map/ppermute | solution.py:23
  83.9 6.3 %collective-permute-start.12 = (bf16[304,1792]{1,0:T(8,128)(2,1)S(1)}, bf16[304,1792]{1,0:T(8,128)(2,1)}, u32[]{:S(2)}, u32[]{:S(2)}) collective-permute-start(bf16[304,1792]{1,0:T(8,128)(2,1)S(1)} %bitcast.61), channel_id=1, source_target_pairs={{0,128},{128,0},{1,129},{129,1},{2,130},{130,2},{3,131},{131,3},{4... | collective-permute-start | bytes 3268616 | tf_op jit(solution)/shard_map/ppermute | solution.py:23
  86.1 3.1 %copy-start.15 = (bf16[304,1792]{1,0:T(8,128)(2,1)}, bf16[304,1792]{1,0:T(8,128)(2,1)S(1)}, u32[]{:S(2)}) copy-start(bf16[304,1792]{1,0:T(8,128)(2,1)S(1)} %collective-permute-done.10.gate_other_ref) | copy-start | bytes 3268612
  89.2 1.0 copy-start.16
  129.3 16.7 %copy-start.22 = (bf16[320,608]{1,0:T(8,128)(2,1)S(1)}, bf16[320,608]{1,0:T(8,128)(2,1)}, u32[]{:S(2)}) copy-start(bf16[320,608]{1,0:T(8,128)(2,1)} %get-tuple-element.62) | copy-start | bytes 1167364
  129.3 45.5 %all-to-all-start.2 = ((bf16[16,16,4608]{2,1,0:T(8,128)(2,1)}), bf16[16,16,4608]{2,1,0:T(8,128)(2,1)S(1)}, u32[]{:S(2)}, u32[]{:S(2)}) async-start(bf16[16,16,4608]{2,1,0:T(8,128)(2,1)} %bitcast.54), calls=%async_computation.2 | async-start | bytes 4718592 | tf_op jit(solution)/shard_map/all_to_all | solution.py:647
  146.0 6.1 %copy-start.6 = (bf16[304,1792]{1,0:T(8,128)(2,1)S(1)}, bf16[304,1792]{1,0:T(8,128)(2,1)}, u32[]{:S(2)}) copy-start(bf16[304,1792]{1,0:T(8,128)(2,1)} %copy-done.5) | copy-start | bytes 3268612
  146.0 6.1 %copy-start.10 = (bf16[608,128]{1,0:T(8,128)(2,1)S(1)}, bf16[608,128]{1,0:T(8,128)(2,1)}, u32[]{:S(2)}) copy-start(bf16[608,128]{1,0:T(8,128)(2,1)} %get-tuple-element.55.backs_ref) | copy-start | bytes 466948
  150.1 2.7 %copy-start.3 = (bf16[304,1792]{1,0:T(8,128)(2,1)S(1)}, bf16[304,1792]{1,0:T(8,128)(2,1)}, u32[]{:S(2)}) copy-start(bf16[304,1792]{1,0:T(8,128)(2,1)} %copy-done.2) | copy-start | bytes 3268612
  150.1 46.7 %collective-permute-start.15 = (bf16[608,1792]{1,0:T(8,128)(2,1)}, bf16[608,1792]{1,0:T(8,128)(2,1)}, u32[]{:S(2)}, u32[]{:S(2)}) collective-permute-start(bf16[608,1792]{1,0:T(8,128)(2,1)} %convolution_convert_fusion), channel_id=1, source_target_pairs={{0,128},{128,0},{1,129},{129,1},{2,130},{130,2},{3,131},{131,3},{4... | collective-permute-start | bytes 6537224 | tf_op jit(solution)/shard_map/ppermute | solution.py:23
  152.8 1.8 copy-start.21
  152.8 2.0 copy-start.24
  154.7 2.4 %copy-start.4 = (bf16[1792,304]{0,1:T(8,128)(2,1)S(1)}, bf16[1792,304]{0,1:T(8,128)(2,1)}, u32[]{:S(2)}) copy-start(bf16[1792,304]{0,1:T(8,128)(2,1)} %param.15) | copy-start | bytes 3268612
  156.5 1.2 copy-start.1
  156.5 37.1 %collective-permute-start.16 = (bf16[304,1792]{1,0:T(8,128)(2,1)}, bf16[304,1792]{1,0:T(8,128)(2,1)S(1)}, u32[]{:S(2)}, u32[]{:S(2)}) collective-permute-start(bf16[304,1792]{1,0:T(8,128)(2,1)} %convolution_convert_fusion.1), channel_id=1, source_target_pairs={{0,128},{128,0},{1,129},{129,1},{2,130},{130,2},{3,131},{131,3},{4... | collective-permute-start | bytes 3268616 | tf_op jit(solution)/shard_map/ppermute | solution.py:23
  174.9 1.4 copy-start
  182.5 32.9 %all-to-all-start.3 = ((bf16[8,464,128]{2,1,0:T(8,128)(2,1)}), bf16[8,464,128]{2,1,0:T(8,128)(2,1)S(1)}, u32[]{:S(2)}, u32[]{:S(2)}) async-start(bf16[8,464,128]{2,1,0:T(8,128)(2,1)} %shard_map.165), calls=%async_computation.3 | async-start | bytes 1900544 | tf_op jit(solution)/shard_map/all_to_all | solution.py:670
  188.4 5.2 %copy-start.25 = (bf16[320,304]{1,0:T(8,128)(2,1)S(1)}, bf16[320,304]{1,0:T(8,128)(2,1)}, u32[]{:S(2)}) copy-start(bf16[320,304]{1,0:T(8,128)(2,1)} %get-tuple-element.64) | copy-start | bytes 583684
  193.6 3.2 %copy-start.20 = (bf16[320,3584]{1,0:T(8,128)(2,1)S(1)}, bf16[320,3584]{1,0:T(8,128)(2,1)}, u32[]{:S(2)}) copy-start(bf16[320,3584]{1,0:T(8,128)(2,1)} %get-tuple-element.63) | copy-start | bytes 6881284
  193.6 3.2 %copy-start.23 = (bf16[320,608]{1,0:T(8,128)(2,1)S(1)}, bf16[320,608]{1,0:T(8,128)(2,1)}, u32[]{:S(2)}) copy-start(bf16[320,608]{1,0:T(8,128)(2,1)} %get-tuple-element.62) | copy-start | bytes 1167364
Sparse Core Ops, SparseCore 0:
  46.7 62.5 all-gather.1
where the time goes:
time: 225 us; the launch traced here: 224 us
  waiting for transfers between devices  78.7 us (35%)
  starting transfers between devices  57.8 us (26%)
  Pallas kernels  41.8 us (19%)
  matrix products  16.1 us (7%)
  between operations  14.2 us (6%)
  local copies, waits for them, and re-layouts  9.8 us (4%)
  other arithmetic  5.24 us (2%)
    all_gather x1, waiting for transfers between devices, local(): lax.all_gather(arrived.reshape(experts * TILE, -1), 'tensor', axis=0, til...  19.2 us
    pallas_call x1, Pallas kernels, expert_rows(): pl.pallas_call(functools.partial(expert_kernel, capacity), grid_spec=pltp...  17 us
    all_to_all x1, starting transfers between devices, local(): lax.all_to_all(sent.reshape(experts, TILE, -1), 'expert', split_axis=0, c...  16.7 us
    dot_general x8, matrix products, product(): return jnp.einsum(spec, left, right, preferred_element_type=F32)  16.1 us
    all_to_all x1, waiting for transfers between devices, local(): lax.all_to_all(sent.reshape(experts, TILE, -1), 'expert', split_axis=0, c...  15.6 us
    ppermute x7, waiting for transfers between devices, ring(): lax.ppermute(values, 'tensor', [(i, (i + shift) % size) for i in range(si...  15.6 us
    all_to_all x1, waiting for transfers between devices, local(): lax.all_to_all(total, 'tensor', split_axis=0, concat_axis=0, tiled=True)  14.2 us
    ppermute x7, starting transfers between devices, ring(): lax.ppermute(values, 'tensor', [(i, (i + shift) % size) for i in range(si...  11.8 us
  transfers between devices with their start and end apart: 22, of which 11 were waited for; matrix products, arithmetic and copies ran while one was open for 11% of the time, Pallas kernels for 19%

commit v1 on v0

--- a/solution.py
+++ b/solution.py
@@ -152,10 +152,9 @@
         down_own_ref,
         down_other_ref,
         own_ref,
+        other_ref,
         backs_ref,
         hidden_ref,
-        pair_terms_ref,
-        down_terms_ref,
         rows,
         arrivals,
         pre,
@@ -167,7 +166,7 @@
     feats = wide // 2
     units = hidden_ref.shape[0]
     block = parts * feats
-    place = lax.rem(coords_ref[1] * 2 + jnp.where(step < 4, step, step - 2), 4)
+    place = lax.rem(coords_ref[1] * 2 + step, 4)
 
     @pl.when(step == 0)
     def _():
@@ -177,15 +176,17 @@
         pre[...] = jnp.zeros_like(pre)
         from_down[...] = jnp.zeros_like(from_down)
 
-    @pl.when(step < 4)
-    def _():
-        for part in range(parts):
-            origin = place * parts + part
-            pltpu.make_async_copy(pieces[0], rows.at[origin], arrivals.at[origin]).wait()
+    for part in range(parts):
+        origin = place * parts + part
+        pltpu.make_async_copy(pieces[0], rows.at[origin], arrivals.at[origin]).wait()
 
     @pl.when(step < 2)
     def _():
         own_ref[...] = rows[pl.ds(place * parts, parts)]
+
+    @pl.when(step >= 2)
+    def _():
+        other_ref[...] = rows[pl.ds(place * parts, parts)]
 
     rows_in = rows[pl.ds(place * parts, parts), :feats, :].reshape(block, tokens)
     rows_out = rows[pl.ds(place * parts, parts), feats:, :].reshape(block, tokens)
@@ -199,7 +200,7 @@
     def _():
         forward(gate_own_ref, up_own_ref, down_own_ref)
 
-    @pl.when((step >= 2) & (step < 4))
+    @pl.when(step >= 2)
     def _():
         forward(gate_other_ref, up_other_ref, down_other_ref)
 
@@ -211,19 +212,6 @@
         hidden_ref[...] = (act * raised).astype(BF16)
         backs_ref[:units] = (back * raised * slope).astype(BF16)
         backs_ref[units:] = (back * act).astype(BF16)
-
-    @pl.when(step >= 4)
-    def _():
-        backs = contract(rows_in, backs_ref[...], 1, 1).astype(BF16)
-        down = contract(rows_out, hidden_ref[...], 1, 1).astype(BF16)
-        empty = pair_terms_ref.shape[1] - 2 * units
-        pair_terms_ref[...] = jnp.concatenate([backs, jnp.zeros((block, empty), BF16)], axis=1)
-        empty = down_terms_ref.shape[1] - units
-        down_terms_ref[...] = jnp.concatenate([down, jnp.zeros((block, empty), BF16)], axis=1)
-
-
-def lane_up(count):
-    return -(-count // LANES) * LANES
 
 
 def dense_forward(pieces, coords, gates, ups, downs):
@@ -235,20 +223,18 @@
     own = lambda i, c: (0, jnp.minimum(i, 1))
     other = lambda i, c: (0, jnp.clip(i - 2, 0, 1))
     whole = lambda shape: pl.BlockSpec(shape, lambda i, c: (0, 0))
-    term = lambda lanes: pl.BlockSpec((block, lanes), lambda i, c: (jnp.maximum(i - 4, 0), 0))
     return pl.pallas_call(
         functools.partial(dense_kernel, [piece[1] for piece in pieces]),
         grid_spec=pltpu.PrefetchScalarGridSpec(
             num_scalar_prefetch=1,
-            grid=(6,),
+            grid=(4,),
             in_specs=[pl.BlockSpec(memory_space=pl.ANY)] * len(pieces)
             + [pl.BlockSpec((units, block), own), pl.BlockSpec((units, block), other)] * 3,
             out_specs=[
                 pl.BlockSpec((parts, wide, tokens), lambda i, c: (jnp.minimum(i, 1), 0, 0)),
+                pl.BlockSpec((parts, wide, tokens), lambda i, c: (jnp.maximum(i - 2, 0), 0, 0)),
                 whole((2 * units, tokens)),
                 whole((units, tokens)),
-                term(lane_up(2 * units)),
-                term(lane_up(units)),
             ],
             scratch_shapes=[
                 pltpu.VMEM((size, wide, tokens), BF16),
@@ -259,56 +245,78 @@
         ),
         out_shape=[
             shape_of((2 * parts, wide, tokens)),
+            shape_of((2 * parts, wide, tokens)),
             shape_of((2 * units, tokens)),
             shape_of((units, tokens)),
-            shape_of((half_width, lane_up(2 * units))),
-            shape_of((half_width, lane_up(units))),
         ],
         compiler_params=params(),
-        cost_estimate=costs(10),
+        cost_estimate=costs(7),
     )(coords, *[piece[0] for piece in pieces], *gates, *ups, *downs)
 
 
-def terms_kernel(both_ref, backs_ref, hidden_ref, pair_arrived_ref, down_arrived_ref, terms_ref):
-    parts, wide, tokens = both_ref.shape
+def terms_kernel(
+    own_ref, arrived_ref, backs_ref, backs_arrived_ref, hidden_ref, hidden_arrived_ref, terms_ref
+):
+    parts, wide, tokens = own_ref.shape
     feats = wide // 2
     units = hidden_ref.shape[0]
     block = parts * feats
-    first = pair_arrived_ref.shape[1]
-    rows_in = both_ref[:, :feats, :].reshape(block, tokens)
-    rows_out = both_ref[:, feats:, :].reshape(block, tokens)
-    backs = contract(rows_in, backs_ref[...], 1, 1) + pair_arrived_ref[:, : 2 * units].astype(F32)
-    down = contract(rows_out, hidden_ref[...], 1, 1) + down_arrived_ref[:, :units].astype(F32)
-    empty = jnp.zeros((block, first - 2 * units), BF16)
-    terms_ref[:, :first] = jnp.concatenate([backs.astype(BF16), empty], axis=1)
-    empty = jnp.zeros((block, terms_ref.shape[1] - first - units), BF16)
-    terms_ref[:, first:] = jnp.concatenate([down.astype(BF16), empty], axis=1)
-
-
-def dense_terms(own, backs, hidden, pair_arrived, down_arrived):
+    strips = terms_ref.shape[0]
+    tall = block // strips
+    tiles, tail = 3 * units // LANES, 3 * units % LANES
+
+    def both_blocks(left, right):
+        return jnp.concatenate([left, right], axis=1)
+
+    rows_in = both_blocks(
+        own_ref[:, :feats, :].reshape(block, tokens), arrived_ref[:, :feats, :].reshape(block, tokens)
+    )
+    rows_out = both_blocks(
+        own_ref[:, feats:, :].reshape(block, tokens), arrived_ref[:, feats:, :].reshape(block, tokens)
+    )
+    backs = both_blocks(backs_ref[...], backs_arrived_ref[...])
+    hidden = both_blocks(hidden_ref[...], hidden_arrived_ref[...])
+    terms = jnp.concatenate(
+        [contract(rows_in, backs, 1, 1).astype(BF16), contract(rows_out, hidden, 1, 1).astype(BF16)],
+        axis=1,
+    )
+    last = contract(hidden[units - tail :], rows_out, 1, 1).astype(BF16)
+    for strip in range(strips):
+        rows = slice(strip * tall, (strip + 1) * tall)
+        for tile in range(tiles):
+            terms_ref[strip, tile * tall : (tile + 1) * tall, :] = terms[
+                rows, tile * LANES : (tile + 1) * LANES
+            ]
+        terms_ref[strip, tiles * tall :, :] = jnp.concatenate(
+            [last[:, rows], jnp.zeros((tail, LANES - tall), BF16)], axis=1
+        )
+
+
+def dense_terms(own, arrived, backs, backs_arrived, hidden, hidden_arrived, experts):
     size, wide, tokens = own.shape
     units = hidden.shape[0]
     parts = size // 2
-    block = parts * wide // 2
-    half_width, first = pair_arrived.shape
-    second = down_arrived.shape[1]
+    tall = size * wide // 2 // experts
+    deep = 3 * units // LANES * tall + 3 * units % LANES
     whole = lambda shape: pl.BlockSpec(shape, lambda i: (0, 0))
-    tall = lambda lanes: pl.BlockSpec((block, lanes), lambda i: (i, 0))
+    rows = pl.BlockSpec((parts, wide, tokens), lambda i: (i, 0, 0))
     return pl.pallas_call(
         terms_kernel,
         grid=(2,),
-        in_specs=[
-            pl.BlockSpec((parts, wide, tokens), lambda i: (i, 0, 0)),
-            whole((2 * units, tokens)),
-            whole((units, tokens)),
-            tall(first),
-            tall(second),
-        ],
-        out_specs=tall(first + second),
-        out_shape=shape_of((half_width, first + second)),
+        in_specs=[rows] * 2 + [whole((2 * units, tokens))] * 2 + [whole((units, tokens))] * 2,
+        out_specs=pl.BlockSpec((experts // 2, deep, LANES), lambda i: (i, 0, 0)),
+        out_shape=shape_of((experts, deep, LANES)),
         compiler_params=params(),
         cost_estimate=costs(5),
-    )(own, backs, hidden, pair_arrived, down_arrived)
+    )(own, arrived, backs, backs_arrived, hidden, hidden_arrived)
+
+
+def unpacked(terms, units, tall):
+    tiles, tail = 3 * units // LANES, 3 * units % LANES
+    whole = terms[: tiles * tall].reshape(tiles, tall, LANES).transpose(1, 0, 2)
+    return jnp.concatenate(
+        [whole.reshape(tall, tiles * LANES), terms[tiles * tall :, :tall].T], axis=1
+    )
 
 
 def expert_kernel(
@@ -506,6 +514,7 @@
     dense_own_ref,
     dense_other_ref,
     total_ref,
+    extra,
 ):
     step = pl.program_id(0)
     quarters = pl.num_programs(0)
@@ -514,31 +523,30 @@
     parts, tall, tokens = total_ref.shape
     feats = tall - TILE
     lane = lax.broadcasted_iota(jnp.int32, (tokens, slots), 1)
-    down = (((0,), (1,)), ((), ()))
-    pick = lambda place: jnp.where(lane == place, 1.0, 0.0).astype(BF16)
-    first = [pick(places_ref[:, k : k + 1]) for k in range(TOP)]
-    shifted = [pick(places_ref[:, TOP + k : TOP + k + 1] + quarter * left) for k in range(TOP)]
-    rows = lax.dot_general(
-        main_ref[...], first[0] + first[1], down, preferred_element_type=F32
-    ) + lax.dot_general(
-        folded_ref[...], shifted[0] + shifted[1], down, preferred_element_type=F32
-    )
+    pick = lambda place: select(lane == place)
+    near = [pick(places_ref[:, k : k + 1]) for k in range(TOP)]
+    far = [places_ref[:, TOP + k : TOP + k + 1] for k in range(TOP)]
+
+    @pl.when(step == 0)
+    def _():
+        probes = []
+        for k in range(TOP):
+            first = contract(probe_ref[...], near[k], 0, 1)
+            second = contract(probe_ref[...], pick(far[k]), 0, 1)
+            probes.append(first[0:1] + first[1:2] + (second[2:3] + second[3:4]))
+        probes = jnp.concatenate(probes, axis=0)
+        high = probes.astype(BF16).astype(F32)
+        empty = jnp.zeros((TILE - 2 * TOP, tokens), F32)
+        extra[...] = jnp.concatenate([high, probes - high, empty], axis=0).astype(BF16)
+
+    shifted = [pick(place + quarter * left) for place in far]
+    rows = jnp.dot(near[0] + near[1], main_ref[...], preferred_element_type=F32)
+    rows += jnp.dot(shifted[0] + shifted[1], folded_ref[...], preferred_element_type=F32)
     dense = jnp.where(step < quarters // 2, dense_own_ref[...], dense_other_ref[...])
-    rows = (dense + rows).astype(BF16)
+    rows = (dense + rows.T).astype(BF16)
     for part in range(parts):
         total_ref[part, :feats, :] = rows[part * feats : (part + 1) * feats]
-    probes = []
-    for k in range(TOP):
-        near = lax.dot_general(probe_ref[...], first[k], down, preferred_element_type=F32)
-        far = pick(places_ref[:, TOP + k : TOP + k + 1])
-        far = lax.dot_general(probe_ref[...], far, down, preferred_element_type=F32)
-        probes.append(near[0:1] + near[1:2] + (far[2:3] + far[3:4]))
-    probes = jnp.concatenate(probes, axis=0)
-    high = probes.astype(BF16).astype(F32)
-    empty = jnp.zeros((TILE - 2 * TOP, tokens), F32)
-    extra = jnp.concatenate([high, probes - high, empty], axis=0).astype(BF16)
-    for part in range(parts):
-        total_ref[part, feats:, :] = extra
+        total_ref[part, feats:, :] = extra[...]
 
 
 def combine(back, coords, places, dense_own, dense_other, size, capacity):
@@ -569,6 +577,7 @@
                 (size // quarters, feats + TILE, tokens),
                 lambda i, c: (lax.rem(c[1] * (quarters // 2) + i, quarters), 0, 0),
             ),
+            scratch_shapes=[pltpu.VMEM((TILE, tokens), BF16)],
         ),
         out_shape=jax.ShapeDtypeStruct((size, feats + TILE, tokens), BF16),
         compiler_params=pltpu.CompilerParams(
@@ -612,21 +621,25 @@
     arrived = lax.all_to_all(
         folded.reshape(experts, TILE, -1), "expert", split_axis=0, concat_axis=0, tiled=True
     )
-    pieces = single_ring(both, range(1, size // 2 + 1))[0] + [(both, 0)]
-    distances = [piece[1] for piece in pieces]
-    arrived, pieces, dense_weights = lax.optimization_barrier(
-        (arrived, [piece[0] for piece in pieces], dense_weights)
-    )
-    pieces = list(zip(pieces, distances))
+    pieces, state = single_ring(both, range(1, size // 2))
+    arrived, state, dense_weights = lax.optimization_barrier((arrived, state, dense_weights))
+    pieces += single_ring(both, [size // 2], state)[0] + [(both, 0)]
     slices = lax.all_gather(
         arrived.reshape(experts * TILE, -1), "tensor", axis=0, tiled=False
     )
 
-    own_rows, dense_backs, dense_hidden, pair_terms, down_terms = dense_forward(
+    own_rows, other_rows, dense_backs, dense_hidden = dense_forward(
         pieces, coords, *dense_weights
     )
-    terms = dense_terms(own_rows, dense_backs, dense_hidden, swap(pair_terms), swap(down_terms))
-    terms = terms.reshape(experts, -1, terms.shape[1])
+    terms = dense_terms(
+        own_rows,
+        swap(other_rows),
+        dense_backs,
+        swap(dense_backs),
+        dense_hidden,
+        swap(dense_hidden),
+        experts,
+    )
     terms = lax.all_to_all(terms, "expert", split_axis=0, concat_axis=0, tiled=True)
     units = dense_hidden.shape[0]
     dense_own, dense_other = [
@@ -640,10 +653,10 @@
     )
     sent, terms = lax.optimization_barrier((sent, terms))
     terms = terms.astype(F32).sum(axis=0).astype(BF16)
-    first = lane_up(2 * units)
+    terms = unpacked(terms, units, own_rows.shape[0] * feats // experts)
     grad_gate = terms[:, :units]
     grad_up = terms[:, units : 2 * units]
-    grad_down = terms[:, first : first + units].T
+    grad_down = terms[:, 2 * units :].T
     back = lax.all_to_all(
         sent.reshape(experts, TILE, -1), "expert", split_axis=0, concat_axis=0, tiled=True
     )

time: 225 us -> 207 us (0.920)
  starting transfers between devices: 57.8 us -> 49.4 us
  waiting for transfers between devices: 78.7 us -> 73.7 us
    all_to_all x1, starting transfers between devices: 16.7 us -> 10.3 us  [local(): lax.all_to_all(sent.reshape(experts, TILE, -1), 'expert', split_axis=0, c...]
    ppermute x10 -> x11, waiting for transfers between devices: 11.1 us -> 7.44 us  [swap(): return lax.ppermute(values, 'dp', [(0, 1), (1, 0)])]
    all_to_all x1, waiting for transfers between devices: 2.91 us -> 0.01 us  [local(): lax.all_to_all(terms, 'expert', split_axis=0, concat_axis=0, tiled=True)]
    pallas_call x1, Pallas kernels: 11 us -> 8.73 us  [dense_forward(): pl.pallas_call(functools.partial(dense_kernel, [piece[1] for piece in pie...]
    unnamed x55 -> x46, local copies, waits for them, and re-layouts: 7.56 us -> 5.37 us
    ppermute x10 -> x11, starting transfers between devices: 9.58 us -> 10.1 us  [swap(): return lax.ppermute(values, 'dp', [(0, 1), (1, 0)])]
  transfers between devices with their start and end apart: 22 -> 23, of which waited for: 11 -> 10; matrix products, arithmetic and copies ran while one was open for 11% -> 11% of each run, Pallas kernels for 19% -> 19%
where the time goes in v1:
time: 207 us; the launch traced here: 206 us
  waiting for transfers between devices  73.7 us (36%)
  starting transfers between devices  49.4 us (24%)
  Pallas kernels  39.6 us (19%)
  matrix products  16.2 us (8%)
  between operations  14.3 us (7%)
  local copies, waits for them, and re-layouts  7.7 us (4%)
  other arithmetic  5.56 us (3%)
    all_gather x1, waiting for transfers between devices, local(): lax.all_gather(arrived.reshape(experts * TILE, -1), 'tensor', axis=0, til...  20.2 us
    pallas_call x1, Pallas kernels, expert_rows(): pl.pallas_call(functools.partial(expert_kernel, capacity), grid_spec=pltp...  17 us
    dot_general x8, matrix products, product(): return jnp.einsum(spec, left, right, preferred_element_type=F32)  16.2 us
    all_to_all x1, waiting for transfers between devices, local(): lax.all_to_all(total, 'tensor', split_axis=0, concat_axis=0, tiled=True)  16.1 us
    all_to_all x1, waiting for transfers between devices, local(): lax.all_to_all(sent.reshape(experts, TILE, -1), 'expert', split_axis=0, c...  15.5 us
    ppermute x7, waiting for transfers between devices, ring(): lax.ppermute(values, 'tensor', [(i, (i + shift) % size) for i in range(si...  14.4 us
    ppermute x7, starting transfers between devices, ring(): lax.ppermute(values, 'tensor', [(i, (i + shift) % size) for i in range(si...  11.2 us
    all_to_all x1, starting transfers between devices, local(): lax.all_to_all(sent.reshape(experts, TILE, -1), 'expert', split_axis=0, c...  10.3 us
  transfers between devices with their start and end apart: 23, of which 10 were waited for; matrix products, arithmetic and copies ran while one was open for 11% of the time, Pallas kernels for 19%

profile of v1, /device:TPU:19, one launch (start us, length us, event | category | flops | bytes accessed | tf_op | source)
XLA Modules:
  0.0 206.4 jit_solution(4909936809599572338)
XLA Ops:
  7.2 0.8 collective-permute-start.6
  7.9 0.1 collective-permute-start.7
  8.0 0.4 collective-permute-start.8
  8.4 1.0 pad_maximum_fusion.both_ref.refs_7_
  9.4 1.7 collective-permute-start
  11.2 4.0 %collective-permute-start.3 = (bf16[896,128]{1,0:T(8,128)(2,1)S(1)}, bf16[896,128]{1,0:T(8,128)(2,1)S(1)}, u32[]{:S(2)}, u32[]{:S(2)}) collective-permute-start(bf16[896,128]{1,0:T(8,128)(2,1)S(1)} %pad_maximum_fusion.both_ref.refs_7_), channel_id=1, source_target_pairs={{0,7},{1,0},{2,1},{3,2},{4,3},{5,4},{6,5},{7,6},{8,15},{9,8},{10,9... | collective-permute-start | bytes 688136 | tf_op jit(solution)/shard_map/ppermute | solution.py:28
  15.2 2.9 %shard_map.161 = (bf16[256,1152]{1,0:T(8,128)(2,1)}, s32[128,4]{1,0:T(8,128)}) custom-call(s32[2,128]{1,0:T(2,128)} %bitcast.71, f32[2,128]{1,0:T(2,128)} %bitcast.72, bf16[896,128]{1,0:T(8,128)(2,1)} %copy-done.9), custom_call_target="tpu_custom_call" | custom-call | flops 1 | bytes 10500000 | tf_op jit(solution)/shard_map/pallas_call | solution.py:134
  18.1 6.7 %all-to-all-start = ((bf16[16,16,1152]{2,1,0:T(8,128)(2,1)}), bf16[16,16,1152]{2,1,0:T(8,128)(2,1)S(1)}, u32[]{:S(2)}, u32[]{:S(2)}) async-start(bf16[16,16,1152]{2,1,0:T(8,128)(2,1)} %bitcast.68), calls=%async_computation | async-start | bytes 1179648 | tf_op jit(solution)/shard_map/all_to_all | solution.py:621
  24.7 0.0 all-gather.2.cloned.1.call-start
  24.8 0.1 collective-permute-start.1
  24.9 2.6 %collective-permute-start.4 = (bf16[896,128]{1,0:T(8,128)(2,1)S(1)}, bf16[896,128]{1,0:T(8,128)(2,1)S(1)}, u32[]{:S(2)}, u32[]{:S(2)}) collective-permute-start(bf16[896,128]{1,0:T(8,128)(2,1)S(1)} %collective-permute-done.3.refs_1_), channel_id=1, source_target_pairs={{0,7},{1,0},{2,1},{3,2},{4,3},{5,4},{6,5},{7,6},{8,15},{9,8},{10,9... | collective-permute-start | bytes 688136 | tf_op jit(solution)/shard_map/ppermute | solution.py:28
  27.6 4.8 %collective-permute-done.1.refs_2_ = bf16[896,128]{1,0:T(8,128)(2,1)} collective-permute-done((bf16[896,128]{1,0:T(8,128)(2,1)S(1)}, bf16[896,128]{1,0:T(8,128)(2,1)}, u32[]{:S(2)}, u32[]{:S(2)}) %collective-permute-start.1) | collective-permute-done | bytes 229408 | tf_op jit(solution)/shard_map/ppermute | solution.py:28
  32.4 2.7 %collective-permute-start.5 = (bf16[896,128]{1,0:T(8,128)(2,1)S(1)}, bf16[896,128]{1,0:T(8,128)(2,1)}, u32[]{:S(2)}, u32[]{:S(2)}) collective-permute-start(bf16[896,128]{1,0:T(8,128)(2,1)S(1)} %collective-permute-done.4.refs_3_), channel_id=1, source_target_pairs={{0,7},{1,0},{2,1},{3,2},{4,3},{5,4},{6,5},{7,6},{8,15},{9,8},{10,9... | collective-permute-start | bytes 688136 | tf_op jit(solution)/shard_map/ppermute | solution.py:28
  35.1 4.1 %collective-permute-done.2.refs_4_ = bf16[896,128]{1,0:T(8,128)(2,1)} collective-permute-done((bf16[896,128]{1,0:T(8,128)(2,1)}, bf16[896,128]{1,0:T(8,128)(2,1)}, u32[]{:S(2)}, u32[]{:S(2)}) %collective-permute-start.2) | collective-permute-done | bytes 229408 | tf_op jit(solution)/shard_map/ppermute | solution.py:28
  39.2 0.0 all-gather.2.cloned.1.call-update
  39.3 0.1 collective-permute-start.12
  39.4 0.8 pad_add_fusion.coords_ref
  40.1 5.5 %collective-permute-done.12.refs_6_ = bf16[896,128]{1,0:T(8,128)(2,1)S(1)} collective-permute-done((bf16[896,128]{1,0:T(8,128)(2,1)}, bf16[896,128]{1,0:T(8,128)(2,1)S(1)}, u32[]{:S(2)}, u32[]{:S(2)}) %collective-permute-start.12) | collective-permute-done | bytes 229408 | tf_op jit(solution)/shard_map/ppermute | solution.py:28
  45.7 0.7 copy-done.15
  46.4 8.7 %shard_map.163 = (bf16[4,896,128]{2,1,0:T(8,128)(2,1)}, bf16[4,896,128]{2,1,0:T(8,128)(2,1)}, bf16[608,128]{1,0:T(8,128)(2,1)}, bf16[304,128]{1,0:T(8,128)(2,1)}) custom-call(s32[2]{0:T(128)} %pad_add_fusion.coords_ref, bf16[896,128]{1,0:T(8,128)(2,1)} %copy-done.12, bf16[896,128]{1,0:T(8,128)(2,1)} %copy-done.13, ...), custom_call_target="tpu_custom_call" | custom-call | flops 1 | bytes 24500000 | tf_op jit(solution)/shard_map/pallas_call | solution.py:226
  55.1 4.2 %collective-permute-start.13 = (bf16[4,896,128]{2,1,0:T(8,128)(2,1)}, bf16[4,896,128]{2,1,0:T(8,128)(2,1)S(1)}, u32[]{:S(2)}, u32[]{:S(2)}) collective-permute-start(bf16[4,896,128]{2,1,0:T(8,128)(2,1)} %get-tuple-element.40), channel_id=1, source_target_pairs={{0,128},{128,0},{1,129},{129,1},{2,130},{130,2},{3,131},{131,3},{4... | collective-permute-start | bytes 2752520 | tf_op jit(solution)/shard_map/ppermute | solution.py:23
  59.3 0.1 collective-permute-start.14
  59.4 0.4 collective-permute-start.15
  59.8 2.1 %collective-permute-done.15.hidden_arrived_ref = bf16[304,128]{1,0:T(8,128)(2,1)S(1)} collective-permute-done((bf16[304,128]{1,0:T(8,128)(2,1)}, bf16[304,128]{1,0:T(8,128)(2,1)S(1)}, u32[]{:S(2)}, u32[]{:S(2)}) %collective-permute-start.15) | collective-permute-done | bytes 77856 | tf_op jit(solution)/shard_map/ppermute | solution.py:23
  62.0 0.6 copy-done.17
  62.6 0.0 copy-done.16
  62.6 0.4 copy-done.11
  63.0 4.5 %shard_map.164 = bf16[16,800,128]{2,1,0:T(8,128)(2,1)} custom-call(bf16[4,896,128]{2,1,0:T(8,128)(2,1)} %get-tuple-element.39.own_ref, bf16[4,896,128]{2,1,0:T(8,128)(2,1)} %copy-done.11, bf16[608,128]{1,0:T(8,128)(2,1)} %get-tuple-element.41.backs_ref, bf16[608,128]{1,0:T(8,128)(2,1)} %copy-done.16, bf16[304,128]{1,0:T(8,128)(2,1)} %get-tuple-element.42.hidden_ref, ...), custom_call_target="tpu_custom_call" | custom-call | flops 1 | bytes 17500000 | tf_op jit(solution)/shard_map/pallas_call | solution.py:303
  67.6 6.7 %all-to-all-start.1 = ((bf16[16,800,128]{2,1,0:T(8,128)(2,1)}), bf16[16,800,128]{2,1,0:T(8,128)(2,1)S(1)}, u32[]{:S(2)}, u32[]{:S(2)}) async-start(bf16[16,800,128]{2,1,0:T(8,128)(2,1)} %shard_map.164), calls=%async_computation.1 | async-start | bytes 6553600 | tf_op jit(solution)/shard_map/all_to_all | solution.py:643
  74.3 0.9 collective-permute-start.10
  75.2 0.1 collective-permute-start.11
  75.3 0.4 collective-permute-start.9
  75.7 2.2 %collective-permute-done.10.up_other_ref = bf16[304,1792]{1,0:T(8,128)(2,1)} collective-permute-done((bf16[304,1792]{1,0:T(8,128)(2,1)}, bf16[304,1792]{1,0:T(8,128)(2,1)}, u32[]{:S(2)}, u32[]{:S(2)}) %collective-permute-start.10) | collective-permute-done | bytes 1089568 | tf_op jit(solution)/shard_map/ppermute | solution.py:23
  77.9 1.6 collective-permute-done.11.down_other_ref
  79.4 1.6 collective-permute-done.9.gate_other_ref
  81.0 20.2 %all-gather.2.cloned.1.call-done.slices_ref = bf16[8,256,1152]{2,1,0:T(8,128)(2,1)} async-done(((bf16[1,256,1152]{2,1,0:T(8,128)(2,1)}), bf16[8,256,1152]{2,1,0:T(8,128)(2,1)}) %all-gather.2.cloned.1.call-update) | async-done | bytes 4718608 | tf_op jit(solution)/shard_map/all_gather | solution.py:627
  101.2 17.0 %shard_map.162 = (bf16[320,3584]{1,0:T(8,128)(2,1)}, bf16[320,3584]{1,0:T(8,128)(2,1)}, bf16[256,4608]{1,0:T(8,128)(2,1)}, bf16[320,304]{1,0:T(8,128)(2,1)}, bf16[320,608]{1,0:T(8,128)(2,1)}) custom-call(s32[2]{0:T(128)} %pad_add_fusion.coords_ref, bf16[8,256,1152]{2,1,0:T(8,128)(2,1)} %all-gather.2.cloned.1.call-done.slices_ref, ...), custom_call_target="tpu_custom_call" | custom-call | flops 1 | bytes 56000000 | tf_op jit(solution)/shard_map/pallas_call | solution.py:473
  118.2 1.7 copy-done.1
  119.9 10.3 %all-to-all-start.2 = ((bf16[16,16,4608]{2,1,0:T(8,128)(2,1)}), bf16[16,16,4608]{2,1,0:T(8,128)(2,1)S(1)}, u32[]{:S(2)}, u32[]{:S(2)}) async-start(bf16[16,16,4608]{2,1,0:T(8,128)(2,1)} %bitcast.58), calls=%async_computation.2 | async-start | bytes 4718592 | tf_op jit(solution)/shard_map/all_to_all | solution.py:660
  130.2 4.1 %convolution_convert_fusion = bf16[608,1792]{1,0:T(8,128)(2,1)} fusion(bf16[320,608]{1,0:T(8,128)(2,1)} %get-tuple-element.46, bf16[320,3584]{1,0:T(8,128)(2,1)} %get-tuple-element.47, s32[]{:T(128)S(6)} %select_n.9), kind=kOutput, calls=%fused_computation.1 | convolution fusion | flops 698392576 | bytes 3735556 | tf_op jit(solution)/shard_map/sh,sd->hd/dot_general | solution.py:19
  134.3 2.1 %collective-permute-start.16 = (bf16[608,1792]{1,0:T(8,128)(2,1)}, bf16[608,1792]{1,0:T(8,128)(2,1)}, u32[]{:S(2)}, u32[]{:S(2)}) collective-permute-start(bf16[608,1792]{1,0:T(8,128)(2,1)} %convolution_convert_fusion), channel_id=1, source_target_pairs={{0,128},{128,0},{1,129},{129,1},{2,130},{130,2},{3,131},{131,3},{4... | collective-permute-start | bytes 6537224 | tf_op jit(solution)/shard_map/ppermute | solution.py:23
  136.4 0.6 fusion.8
  137.0 1.5 convolution_add_fusion.1.dense_other_ref
  138.5 0.2 copy-done.19
  138.8 0.2 copy-done.21
  138.9 1.7 convolution_convert_fusion.1
  140.7 0.6 collective-permute-start.17
  141.3 0.6 fusion.10
  141.9 1.5 convolution_add_fusion.2.dense_own_ref
  143.4 15.5 %all-to-all-done.2 = bf16[16,16,4608]{2,1,0:T(8,128)(2,1)S(1)} async-done(((bf16[16,16,4608]{2,1,0:T(8,128)(2,1)}), bf16[16,16,4608]{2,1,0:T(8,128)(2,1)S(1)}, u32[]{:S(2)}, u32[]{:S(2)}) %all-to-all-start.2) | async-done | bytes 2359328 | tf_op jit(solution)/shard_map/all_to_all | solution.py:660
  159.0 1.4 copy-done
  160.4 6.4 %shard_map.165 = bf16[8,464,128]{2,1,0:T(8,128)(2,1)} custom-call(s32[2]{0:T(128)} %pad_add_fusion.coords_ref, bf16[256,4608]{1,0:T(8,128)(2,1)} %bitcast.49, bf16[256,4608]{1,0:T(8,128)(2,1)} %bitcast.50, bf16[256,4608]{1,0:T(8,128)(2,1)} %bitcast.51, s32[128,4]{1,0:T(8,128)} %get-tuple-element.44.places_ref, ...), custom_call_target="tpu_custom_call" | custom-call | flops 1 | bytes 21000000 | tf_op jit(solution)/shard_map/pallas_call | solution.py:561
  166.8 4.4 %all-to-all-start.3 = ((bf16[8,464,128]{2,1,0:T(8,128)(2,1)}), bf16[8,464,128]{2,1,0:T(8,128)(2,1)S(1)}, u32[]{:S(2)}, u32[]{:S(2)}) async-start(bf16[8,464,128]{2,1,0:T(8,128)(2,1)} %shard_map.165), calls=%async_computation.3 | async-start | bytes 1900544 | tf_op jit(solution)/shard_map/all_to_all | solution.py:683
  171.2 2.4 %reduce_sum.22 = bf16[800,128]{1,0:T(8,128)(2,1)S(1)} reduce(bf16[16,800,128]{2,1,0:T(8,128)(2,1)} %copy-done.1, bf16[]{:T(256)} %constant.6.clone.1), dimensions={0}, to_apply=%region_1.0 | reduce | flops 1536000 | bytes 3481602 | tf_op jit(solution)/shard_map/reduce_sum | solution.py:655
  173.6 0.2 copy.19
  173.8 0.7 fusion.7
  174.5 0.0 copy-done.22
  174.5 3.2 %fusion.1 = bf16[1,304,1792]{2,1,0:T(8,128)(2,1)} fusion(bf16[320,304]{1,0:T(8,128)(2,1)S(1)} %copy-done.22, bf16[304,1792]{1,0:T(8,128)(2,1)S(1)} %collective-permute-done.17, bf16[320,3584]{1,0:T(8,128)(2,1)} %get-tuple-element.49, s32[]{:T(128)S(6)} %select_n.8), kind=kOutput, calls=%fused_computation.5 | convolution fusion | flops 350285824 | bytes 3520516 | tf_op jit(solution)/shard_map/sh,sd->hd/dot_general | solution.py:19
  177.7 3.0 %add_convert_fusion = bf16[608,1792]{1,0:T(8,128)(2,1)S(1)} fusion(bf16[608,1792]{1,0:T(8,128)(2,1)} %collective-permute-done.16, bf16[320,608]{1,0:T(8,128)(2,1)S(1)} %copy-done.20, bf16[320,3584]{1,0:T(8,128)(2,1)S(1)} %copy-done.18, s32[]{:T(128)S(6)} %select_n.8), kind=kOutput, calls=%fused_computation | convolution fusion | flops 700571648 | bytes 5914628 | tf_op jit(solution)/shard_map/sh,sd->hd/dot_general | solution.py:19
  180.7 1.5 slice_bitcast_fusion
  182.1 16.1 %all-to-all-done.3 = bf16[8,464,128]{2,1,0:T(8,128)(2,1)S(1)} async-done(((bf16[8,464,128]{2,1,0:T(8,128)(2,1)}), bf16[8,464,128]{2,1,0:T(8,128)(2,1)S(1)}, u32[]{:S(2)}, u32[]{:S(2)}) %all-to-all-start.3) | async-done | bytes 950304 | tf_op jit(solution)/shard_map/all_to_all | solution.py:683
  198.2 0.1 convert_reduce_fusion
  198.4 0.7 fusion.6
  199.0 0.6 fusion.14
  (53 shorter events, 0.1 us)
Async XLA Ops:
  7.2 32.0 %collective-permute-start.6 = (bf16[304,1792]{1,0:T(8,128)(2,1)}, bf16[304,1792]{1,0:T(8,128)(2,1)S(1)}, u32[]{:S(2)}, u32[]{:S(2)}) collective-permute-start(bf16[304,1792]{1,0:T(8,128)(2,1)} %bitcast.52), channel_id=1, source_target_pairs={{0,128},{128,0},{1,129},{129,1},{2,130},{130,2},{3,131},{131,3},{4... | collective-permute-start | bytes 3268616 | tf_op jit(solution)/shard_map/ppermute | solution.py:23
  7.9 31.3 %collective-permute-start.7 = (bf16[304,1792]{1,0:T(8,128)(2,1)}, bf16[304,1792]{1,0:T(8,128)(2,1)S(1)}, u32[]{:S(2)}, u32[]{:S(2)}) collective-permute-start(bf16[304,1792]{1,0:T(8,128)(2,1)} %bitcast.55), channel_id=1, source_target_pairs={{0,128},{128,0},{1,129},{129,1},{2,130},{130,2},{3,131},{131,3},{4... | collective-permute-start | bytes 3268616 | tf_op jit(solution)/shard_map/ppermute | solution.py:23
  8.0 31.2 %collective-permute-start.8 = (bf16[304,1792]{1,0:T(8,128)(2,1)}, bf16[304,1792]{1,0:T(8,128)(2,1)}, u32[]{:S(2)}, u32[]{:S(2)}) collective-permute-start(bf16[304,1792]{1,0:T(8,128)(2,1)} %refs_12_), channel_id=1, source_target_pairs={{0,128},{128,0},{1,129},{129,1},{2,130},{130,2},{3,131},{131,3},{4... | collective-permute-start | bytes 3268616 | tf_op jit(solution)/shard_map/ppermute | solution.py:23
  9.4 5.8 %copy-start.9 = (bf16[896,128]{1,0:T(8,128)(2,1)}, bf16[896,128]{1,0:T(8,128)(2,1)S(1)}, u32[]{:S(2)}) copy-start(bf16[896,128]{1,0:T(8,128)(2,1)S(1)} %pad_maximum_fusion.both_ref.refs_7_) | copy-start | bytes 688132
  9.4 15.4 %collective-permute-start = (bf16[896,128]{1,0:T(8,128)(2,1)S(1)}, bf16[896,128]{1,0:T(8,128)(2,1)S(1)}, u32[]{:S(2)}, u32[]{:S(2)}) collective-permute-start(bf16[896,128]{1,0:T(8,128)(2,1)S(1)} %pad_maximum_fusion.both_ref.refs_7_), channel_id=1, source_target_pairs={{0,1},{1,2},{2,3},{3,4},{4,5},{5,6},{6,7},{7,0},{8,9},{9,10},{10,1... | collective-permute-start | bytes 688136 | tf_op jit(solution)/shard_map/ppermute | solution.py:28
  11.2 13.7 %collective-permute-start.3 = (bf16[896,128]{1,0:T(8,128)(2,1)S(1)}, bf16[896,128]{1,0:T(8,128)(2,1)S(1)}, u32[]{:S(2)}, u32[]{:S(2)}) collective-permute-start(bf16[896,128]{1,0:T(8,128)(2,1)S(1)} %pad_maximum_fusion.both_ref.refs_7_), channel_id=1, source_target_pairs={{0,7},{1,0},{2,1},{3,2},{4,3},{5,4},{6,5},{7,6},{8,15},{9,8},{10,9... | collective-permute-start | bytes 688136 | tf_op jit(solution)/shard_map/ppermute | solution.py:28
  18.1 17.0 %all-to-all-start = ((bf16[16,16,1152]{2,1,0:T(8,128)(2,1)}), bf16[16,16,1152]{2,1,0:T(8,128)(2,1)S(1)}, u32[]{:S(2)}, u32[]{:S(2)}) async-start(bf16[16,16,1152]{2,1,0:T(8,128)(2,1)} %bitcast.68), calls=%async_computation | async-start | bytes 1179648 | tf_op jit(solution)/shard_map/all_to_all | solution.py:621
  24.7 76.4 %all-gather.2.cloned.1.call-start = ((), (), s32[]{:S(2)}) async-start(), calls=%async_computation.4 | async-start | bytes 5308416 | tf_op jit(solution)/shard_map/all_gather | solution.py:627
  24.8 20.8 %copy-start.12 = (bf16[896,128]{1,0:T(8,128)(2,1)}, bf16[896,128]{1,0:T(8,128)(2,1)S(1)}, u32[]{:S(2)}) copy-start(bf16[896,128]{1,0:T(8,128)(2,1)S(1)} %collective-permute-done.refs_0_) | copy-start | bytes 688132
  24.8 7.6 %collective-permute-start.1 = (bf16[896,128]{1,0:T(8,128)(2,1)S(1)}, bf16[896,128]{1,0:T(8,128)(2,1)}, u32[]{:S(2)}, u32[]{:S(2)}) collective-permute-start(bf16[896,128]{1,0:T(8,128)(2,1)S(1)} %collective-permute-done.refs_0_), channel_id=1, source_target_pairs={{0,1},{1,2},{2,3},{3,4},{4,5},{5,6},{6,7},{7,0},{8,9},{9,10},{10,1... | collective-permute-start | bytes 688136 | tf_op jit(solution)/shard_map/ppermute | solution.py:28
  24.9 20.7 %copy-start.13 = (bf16[896,128]{1,0:T(8,128)(2,1)}, bf16[896,128]{1,0:T(8,128)(2,1)S(1)}, u32[]{:S(2)}) copy-start(bf16[896,128]{1,0:T(8,128)(2,1)S(1)} %collective-permute-done.3.refs_1_) | copy-start | bytes 688132
  24.9 7.5 %collective-permute-start.4 = (bf16[896,128]{1,0:T(8,128)(2,1)S(1)}, bf16[896,128]{1,0:T(8,128)(2,1)S(1)}, u32[]{:S(2)}, u32[]{:S(2)}) collective-permute-start(bf16[896,128]{1,0:T(8,128)(2,1)S(1)} %collective-permute-done.3.refs_1_), channel_id=1, source_target_pairs={{0,7},{1,0},{2,1},{3,2},{4,3},{5,4},{6,5},{7,6},{8,15},{9,8},{10,9... | collective-permute-start | bytes 688136 | tf_op jit(solution)/shard_map/ppermute | solution.py:28
  32.4 6.8 %collective-permute-start.2 = (bf16[896,128]{1,0:T(8,128)(2,1)}, bf16[896,128]{1,0:T(8,128)(2,1)}, u32[]{:S(2)}, u32[]{:S(2)}) collective-permute-start(bf16[896,128]{1,0:T(8,128)(2,1)} %collective-permute-done.1.refs_2_), channel_id=1, source_target_pairs={{0,1},{1,2},{2,3},{3,4},{4,5},{5,6},{6,7},{7,0},{8,9},{9,10},{10,1... | collective-permute-start | bytes 688136 | tf_op jit(solution)/shard_map/ppermute | solution.py:28
  32.4 13.2 %copy-start.14 = (bf16[896,128]{1,0:T(8,128)(2,1)}, bf16[896,128]{1,0:T(8,128)(2,1)S(1)}, u32[]{:S(2)}) copy-start(bf16[896,128]{1,0:T(8,128)(2,1)S(1)} %collective-permute-done.4.refs_3_) | copy-start | bytes 688132
  32.4 6.8 %collective-permute-start.5 = (bf16[896,128]{1,0:T(8,128)(2,1)S(1)}, bf16[896,128]{1,0:T(8,128)(2,1)}, u32[]{:S(2)}, u32[]{:S(2)}) collective-permute-start(bf16[896,128]{1,0:T(8,128)(2,1)S(1)} %collective-permute-done.4.refs_3_), channel_id=1, source_target_pairs={{0,7},{1,0},{2,1},{3,2},{4,3},{5,4},{6,5},{7,6},{8,15},{9,8},{10,9... | collective-permute-start | bytes 688136 | tf_op jit(solution)/shard_map/ppermute | solution.py:28
  35.1 4.2 %copy-start.8 = (bf16[16,16,1152]{2,1,0:T(8,128)(2,1)}, bf16[16,16,1152]{2,1,0:T(8,128)(2,1)S(1)}, u32[]{:S(2)}) copy-start(bf16[16,16,1152]{2,1,0:T(8,128)(2,1)S(1)} %all-to-all-done) | copy-start | bytes 1769476
  39.2 6.5 %copy-start.3 = (bf16[304,1792]{1,0:T(8,128)(2,1)}, bf16[304,1792]{1,0:T(8,128)(2,1)S(1)}, u32[]{:S(2)}) copy-start(bf16[304,1792]{1,0:T(8,128)(2,1)S(1)} %collective-permute-done.6.refs_9_) | copy-start | bytes 3268612
  39.2 6.5 %copy-start.6 = (bf16[304,1792]{1,0:T(8,128)(2,1)}, bf16[304,1792]{1,0:T(8,128)(2,1)S(1)}, u32[]{:S(2)}) copy-start(bf16[304,1792]{1,0:T(8,128)(2,1)S(1)} %collective-permute-done.7.refs_11_) | copy-start | bytes 3268612
  39.3 6.4 %collective-permute-start.12 = (bf16[896,128]{1,0:T(8,128)(2,1)}, bf16[896,128]{1,0:T(8,128)(2,1)S(1)}, u32[]{:S(2)}, u32[]{:S(2)}) collective-permute-start(bf16[896,128]{1,0:T(8,128)(2,1)} %collective-permute-done.2.refs_4_), channel_id=1, source_target_pairs={{0,1},{1,2},{2,3},{3,4},{4,5},{5,6},{6,7},{7,0},{8,9},{9,10},{10,1... | collective-permute-start | bytes 688136 | tf_op jit(solution)/shard_map/ppermute | solution.py:28
  45.7 0.7 copy-start.15
  55.1 6.8 %collective-permute-start.13 = (bf16[4,896,128]{2,1,0:T(8,128)(2,1)}, bf16[4,896,128]{2,1,0:T(8,128)(2,1)S(1)}, u32[]{:S(2)}, u32[]{:S(2)}) collective-permute-start(bf16[4,896,128]{2,1,0:T(8,128)(2,1)} %get-tuple-element.40), channel_id=1, source_target_pairs={{0,128},{128,0},{1,129},{129,1},{2,130},{130,2},{3,131},{131,3},{4... | collective-permute-start | bytes 2752520 | tf_op jit(solution)/shard_map/ppermute | solution.py:23
  59.3 2.6 %collective-permute-start.14 = (bf16[608,128]{1,0:T(8,128)(2,1)}, bf16[608,128]{1,0:T(8,128)(2,1)S(1)}, u32[]{:S(2)}, u32[]{:S(2)}) collective-permute-start(bf16[608,128]{1,0:T(8,128)(2,1)} %get-tuple-element.41.backs_ref), channel_id=1, source_target_pairs={{0,128},{128,0},{1,129},{129,1},{2,130},{130,2},{3,131},{131,3},{4... | collective-permute-start | bytes 466952 | tf_op jit(solution)/shard_map/ppermute | solution.py:23
  59.4 2.5 %collective-permute-start.15 = (bf16[304,128]{1,0:T(8,128)(2,1)}, bf16[304,128]{1,0:T(8,128)(2,1)S(1)}, u32[]{:S(2)}, u32[]{:S(2)}) collective-permute-start(bf16[304,128]{1,0:T(8,128)(2,1)} %get-tuple-element.42.hidden_ref), channel_id=1, source_target_pairs={{0,128},{128,0},{1,129},{129,1},{2,130},{130,2},{3,131},{131,3},{4... | collective-permute-start | bytes 233480 | tf_op jit(solution)/shard_map/ppermute | solution.py:23
  62.0 0.6 copy-start.17
  62.0 0.7 copy-start.16
  62.0 1.1 copy-start.11
  67.6 50.6 %all-to-all-start.1 = ((bf16[16,800,128]{2,1,0:T(8,128)(2,1)}), bf16[16,800,128]{2,1,0:T(8,128)(2,1)S(1)}, u32[]{:S(2)}, u32[]{:S(2)}) async-start(bf16[16,800,128]{2,1,0:T(8,128)(2,1)} %shard_map.164), calls=%async_computation.1 | async-start | bytes 6553600 | tf_op jit(solution)/shard_map/all_to_all | solution.py:643
  74.3 3.6 %collective-permute-start.10 = (bf16[304,1792]{1,0:T(8,128)(2,1)}, bf16[304,1792]{1,0:T(8,128)(2,1)}, u32[]{:S(2)}, u32[]{:S(2)}) collective-permute-start(bf16[304,1792]{1,0:T(8,128)(2,1)} %bitcast.63), channel_id=1, source_target_pairs={{0,128},{128,0},{1,129},{129,1},{2,130},{130,2},{3,131},{131,3},{4... | collective-permute-start | bytes 3268616 | tf_op jit(solution)/shard_map/ppermute | solution.py:23
  75.2 4.2 %collective-permute-start.11 = (bf16[304,1792]{1,0:T(8,128)(2,1)}, bf16[304,1792]{1,0:T(8,128)(2,1)}, u32[]{:S(2)}, u32[]{:S(2)}) collective-permute-start(bf16[304,1792]{1,0:T(8,128)(2,1)} %bitcast.65), channel_id=1, source_target_pairs={{0,128},{128,0},{1,129},{129,1},{2,130},{130,2},{3,131},{131,3},{4... | collective-permute-start | bytes 3268616 | tf_op jit(solution)/shard_map/ppermute | solution.py:23
  75.3 5.7 %collective-permute-start.9 = (bf16[304,1792]{1,0:T(8,128)(2,1)}, bf16[304,1792]{1,0:T(8,128)(2,1)}, u32[]{:S(2)}, u32[]{:S(2)}) collective-permute-start(bf16[304,1792]{1,0:T(8,128)(2,1)} %bitcast.61), channel_id=1, source_target_pairs={{0,128},{128,0},{1,129},{129,1},{2,130},{130,2},{3,131},{131,3},{4... | collective-permute-start | bytes 3268616 | tf_op jit(solution)/shard_map/ppermute | solution.py:23
  118.2 1.7 copy-start.1
  119.9 39.1 %all-to-all-start.2 = ((bf16[16,16,4608]{2,1,0:T(8,128)(2,1)}), bf16[16,16,4608]{2,1,0:T(8,128)(2,1)S(1)}, u32[]{:S(2)}, u32[]{:S(2)}) async-start(bf16[16,16,4608]{2,1,0:T(8,128)(2,1)} %bitcast.58), calls=%async_computation.2 | async-start | bytes 4718592 | tf_op jit(solution)/shard_map/all_to_all | solution.py:660
  130.1 6.2 %copy-start.7 = (bf16[304,1792]{1,0:T(8,128)(2,1)S(1)}, bf16[304,1792]{1,0:T(8,128)(2,1)}, u32[]{:S(2)}) copy-start(bf16[304,1792]{1,0:T(8,128)(2,1)} %copy-done.6) | copy-start | bytes 3268612
  130.2 6.2 %copy-start.10 = (bf16[608,128]{1,0:T(8,128)(2,1)S(1)}, bf16[608,128]{1,0:T(8,128)(2,1)}, u32[]{:S(2)}) copy-start(bf16[608,128]{1,0:T(8,128)(2,1)} %get-tuple-element.41.backs_ref) | copy-start | bytes 466948
  134.3 2.7 %copy-start.4 = (bf16[304,1792]{1,0:T(8,128)(2,1)S(1)}, bf16[304,1792]{1,0:T(8,128)(2,1)}, u32[]{:S(2)}) copy-start(bf16[304,1792]{1,0:T(8,128)(2,1)} %copy-done.3) | copy-start | bytes 3268612
  134.3 43.4 %collective-permute-start.16 = (bf16[608,1792]{1,0:T(8,128)(2,1)}, bf16[608,1792]{1,0:T(8,128)(2,1)}, u32[]{:S(2)}, u32[]{:S(2)}) collective-permute-start(bf16[608,1792]{1,0:T(8,128)(2,1)} %convolution_convert_fusion), channel_id=1, source_target_pairs={{0,128},{128,0},{1,129},{129,1},{2,130},{130,2},{3,131},{131,3},{4... | collective-permute-start | bytes 6537224 | tf_op jit(solution)/shard_map/ppermute | solution.py:23
  137.0 1.8 copy-start.19
  137.0 2.0 copy-start.21
  138.9 2.4 %copy-start.5 = (bf16[1792,304]{0,1:T(8,128)(2,1)S(1)}, bf16[1792,304]{0,1:T(8,128)(2,1)}, u32[]{:S(2)}) copy-start(bf16[1792,304]{0,1:T(8,128)(2,1)} %param.15) | copy-start | bytes 3268612
  140.7 1.2 copy-start.2
  140.7 33.8 %collective-permute-start.17 = (bf16[304,1792]{1,0:T(8,128)(2,1)}, bf16[304,1792]{1,0:T(8,128)(2,1)S(1)}, u32[]{:S(2)}, u32[]{:S(2)}) collective-permute-start(bf16[304,1792]{1,0:T(8,128)(2,1)} %convolution_convert_fusion.1), channel_id=1, source_target_pairs={{0,128},{128,0},{1,129},{129,1},{2,130},{130,2},{3,131},{131,3},{4... | collective-permute-start | bytes 3268616 | tf_op jit(solution)/shard_map/ppermute | solution.py:23
  159.0 1.4 copy-start
  166.8 31.5 %all-to-all-start.3 = ((bf16[8,464,128]{2,1,0:T(8,128)(2,1)}), bf16[8,464,128]{2,1,0:T(8,128)(2,1)S(1)}, u32[]{:S(2)}, u32[]{:S(2)}) async-start(bf16[8,464,128]{2,1,0:T(8,128)(2,1)} %shard_map.165), calls=%async_computation.3 | async-start | bytes 1900544 | tf_op jit(solution)/shard_map/all_to_all | solution.py:683
  173.6 0.9 copy-start.22
  174.5 3.2 %copy-start.18 = (bf16[320,3584]{1,0:T(8,128)(2,1)S(1)}, bf16[320,3584]{1,0:T(8,128)(2,1)}, u32[]{:S(2)}) copy-start(bf16[320,3584]{1,0:T(8,128)(2,1)} %get-tuple-element.47) | copy-start | bytes 6881284
  174.5 3.2 %copy-start.20 = (bf16[320,608]{1,0:T(8,128)(2,1)S(1)}, bf16[320,608]{1,0:T(8,128)(2,1)}, u32[]{:S(2)}) copy-start(bf16[320,608]{1,0:T(8,128)(2,1)} %get-tuple-element.46) | copy-start | bytes 1167364
Sparse Core Ops, SparseCore 0:
  39.4 61.7 all-gather.1

commit v2 on v1

--- a/solution.py
+++ b/solution.py
@@ -338,6 +338,7 @@
     from_down,
     folded,
     scale,
+    folds,
 ):
     step = pl.program_id(0)
     quarters = pl.num_programs(0) // 2
@@ -351,17 +352,16 @@
     owned = lax.rem(step, quarters) < quarters // 2
     place = lax.rem(coords_ref[1] * (quarters // 2) + step, quarters)
 
-    source = lax.broadcasted_iota(jnp.int32, (main, rest), 1)
-    target = lax.broadcasted_iota(jnp.int32, (main, rest), 0)
-
-    def fold(quarter):
-        return select(target == source // left * TILE + quarter * left + source % left)
-
     @pl.when(step == 0)
     def _():
         pre[...] = jnp.zeros_like(pre)
         from_down[...] = jnp.zeros_like(from_down)
         folded[...] = jnp.zeros_like(folded)
+        source = lax.broadcasted_iota(jnp.int32, (main, rest), 1)
+        target = lax.broadcasted_iota(jnp.int32, (main, rest), 0)
+        first = source // left * TILE + source % left
+        for quarter in range(quarters):
+            folds[quarter] = select(target == first + quarter * left)
 
     def forward(gate_ref, up_ref, down_ref):
         pair_rows = jnp.concatenate([gate_ref[...], up_ref[...]], axis=0)
@@ -371,14 +371,14 @@
         def _():
             scales = parts[0][:, 2 * feats + piece :]
             scale[:main] = scales[:, 0:1].astype(F32)
-            scale[main:] = contract(fold(0), scales, 0, 0)[:, 1:2]
+            scale[main:] = contract(folds[0], scales, 0, 0)[:, 1:2]
 
         rows_in_ref[:main] = jnp.concatenate([part[:, :feats] for part in parts], axis=1)
         rows_out = jnp.concatenate([part[:, feats : 2 * feats] for part in parts], axis=1)
         beside = jnp.concatenate(
             [part[:, 2 * feats : 2 * feats + piece] for part in parts], axis=1
         )
-        spread = [contract(fold(quarter), beside, 0, 0).astype(BF16) for quarter in range(quarters)]
+        spread = [contract(folds[quarter], beside, 0, 0).astype(BF16) for quarter in range(quarters)]
         half = quarters // 2
 
         def unfolded(which):
@@ -423,14 +423,14 @@
         beside = jnp.where(lane == 0, high[:main], jnp.where(lane == 1, low[:main], 0.0))
         lane = lax.broadcasted_iota(jnp.int32, (rest, LANES), 1)
         after = jnp.where(lane == 2, high[main:], jnp.where(lane == 3, low[main:], 0.0))
-        after = jnp.dot(fold(0), after.astype(BF16), preferred_element_type=F32)
+        after = jnp.dot(folds[0], after.astype(BF16), preferred_element_type=F32)
         sent_ref[:, sent_ref.shape[1] - LANES :] = (beside + after).astype(BF16)
 
     def backward(gate_ref, up_ref):
         pair_rows = jnp.concatenate([gate_ref[...], up_ref[...]], axis=0)
         rows = jnp.dot(backs_ref[...], pair_rows, preferred_element_type=F32).astype(BF16)
         sent_ref[:, pl.ds(pl.multiple_of(place * block, LANES), block)] = rows[:main]
-        folded[...] += jnp.dot(fold(place), rows[main:], preferred_element_type=F32)
+        folded[...] += jnp.dot(folds[place], rows[main:], preferred_element_type=F32)
 
     @pl.when((step >= quarters) & owned)
     def _():
@@ -490,6 +490,7 @@
                 pltpu.VMEM((rows, units), F32),
                 pltpu.VMEM((main, block), F32),
                 pltpu.VMEM((rows, 1), F32),
+                pltpu.VMEM((quarters, main, rows - main), BF16),
             ],
         ),
         out_shape=[

time: 207 us -> 207 us (level)
  no operation moved by 1% of the time
where the time goes in v2:
time: 207 us; the launch traced here: 206 us
  waiting for transfers between devices  73.7 us (36%)
  starting transfers between devices  49.3 us (24%)
  Pallas kernels  39.6 us (19%)
  matrix products  16.2 us (8%)
  between operations  14.3 us (7%)
  local copies, waits for them, and re-layouts  7.7 us (4%)
  other arithmetic  5.56 us (3%)
    all_gather x1, waiting for transfers between devices, local(): lax.all_gather(arrived.reshape(experts * TILE, -1), 'tensor', axis=0, til...  20.2 us
    pallas_call x1, Pallas kernels, expert_rows(): pl.pallas_call(functools.partial(expert_kernel, capacity), grid_spec=pltp...  17 us
    dot_general x8, matrix products, product(): return jnp.einsum(spec, left, right, preferred_element_type=F32)  16.2 us
    all_to_all x1, waiting for transfers between devices, local(): lax.all_to_all(total, 'tensor', split_axis=0, concat_axis=0, tiled=True)  16.1 us
    all_to_all x1, waiting for transfers between devices, local(): lax.all_to_all(sent.reshape(experts, TILE, -1), 'expert', split_axis=0, c...  15.5 us
    ppermute x7, waiting for transfers between devices, ring(): lax.ppermute(values, 'tensor', [(i, (i + shift) % size) for i in range(si...  14.4 us
    ppermute x7, starting transfers between devices, ring(): lax.ppermute(values, 'tensor', [(i, (i + shift) % size) for i in range(si...  11.2 us
    all_to_all x1, starting transfers between devices, local(): lax.all_to_all(sent.reshape(experts, TILE, -1), 'expert', split_axis=0, c...  10.2 us
  transfers between devices with their start and end apart: 23, of which 10 were waited for; matrix products, arithmetic and copies ran while one was open for 11% of the time, Pallas kernels for 19%

profile of v2, /device:TPU:19, one launch (start us, length us, event | category | flops | bytes accessed | tf_op | source)
XLA Modules:
  0.0 206.4 jit_solution(13747634549655774957)
XLA Ops:
  7.2 0.8 collective-permute-start.6
  7.9 0.1 collective-permute-start.7
  8.0 0.4 collective-permute-start.8
  8.4 1.0 pad_maximum_fusion.both_ref.refs_7_
  9.4 1.7 collective-permute-start
  11.2 4.0 %collective-permute-start.3 = (bf16[896,128]{1,0:T(8,128)(2,1)S(1)}, bf16[896,128]{1,0:T(8,128)(2,1)S(1)}, u32[]{:S(2)}, u32[]{:S(2)}) collective-permute-start(bf16[896,128]{1,0:T(8,128)(2,1)S(1)} %pad_maximum_fusion.both_ref.refs_7_), channel_id=1, source_target_pairs={{0,7},{1,0},{2,1},{3,2},{4,3},{5,4},{6,5},{7,6},{8,15},{9,8},{10,9... | collective-permute-start | bytes 688136 | tf_op jit(solution)/shard_map/ppermute | solution.py:28
  15.2 2.9 %shard_map.161 = (bf16[256,1152]{1,0:T(8,128)(2,1)}, s32[128,4]{1,0:T(8,128)}) custom-call(s32[2,128]{1,0:T(2,128)} %bitcast.71, f32[2,128]{1,0:T(2,128)} %bitcast.72, bf16[896,128]{1,0:T(8,128)(2,1)} %copy-done.9), custom_call_target="tpu_custom_call" | custom-call | flops 1 | bytes 10500000 | tf_op jit(solution)/shard_map/pallas_call | solution.py:134
  18.1 6.7 %all-to-all-start = ((bf16[16,16,1152]{2,1,0:T(8,128)(2,1)}), bf16[16,16,1152]{2,1,0:T(8,128)(2,1)S(1)}, u32[]{:S(2)}, u32[]{:S(2)}) async-start(bf16[16,16,1152]{2,1,0:T(8,128)(2,1)} %bitcast.68), calls=%async_computation | async-start | bytes 1179648 | tf_op jit(solution)/shard_map/all_to_all | solution.py:622
  24.7 0.0 all-gather.2.cloned.1.call-start
  24.8 0.1 collective-permute-start.1
  24.9 2.6 %collective-permute-start.4 = (bf16[896,128]{1,0:T(8,128)(2,1)S(1)}, bf16[896,128]{1,0:T(8,128)(2,1)S(1)}, u32[]{:S(2)}, u32[]{:S(2)}) collective-permute-start(bf16[896,128]{1,0:T(8,128)(2,1)S(1)} %collective-permute-done.3.refs_1_), channel_id=1, source_target_pairs={{0,7},{1,0},{2,1},{3,2},{4,3},{5,4},{6,5},{7,6},{8,15},{9,8},{10,9... | collective-permute-start | bytes 688136 | tf_op jit(solution)/shard_map/ppermute | solution.py:28
  27.6 4.8 %collective-permute-done.1.refs_2_ = bf16[896,128]{1,0:T(8,128)(2,1)} collective-permute-done((bf16[896,128]{1,0:T(8,128)(2,1)S(1)}, bf16[896,128]{1,0:T(8,128)(2,1)}, u32[]{:S(2)}, u32[]{:S(2)}) %collective-permute-start.1) | collective-permute-done | bytes 229408 | tf_op jit(solution)/shard_map/ppermute | solution.py:28
  32.4 2.7 %collective-permute-start.5 = (bf16[896,128]{1,0:T(8,128)(2,1)S(1)}, bf16[896,128]{1,0:T(8,128)(2,1)}, u32[]{:S(2)}, u32[]{:S(2)}) collective-permute-start(bf16[896,128]{1,0:T(8,128)(2,1)S(1)} %collective-permute-done.4.refs_3_), channel_id=1, source_target_pairs={{0,7},{1,0},{2,1},{3,2},{4,3},{5,4},{6,5},{7,6},{8,15},{9,8},{10,9... | collective-permute-start | bytes 688136 | tf_op jit(solution)/shard_map/ppermute | solution.py:28
  35.1 4.1 %collective-permute-done.2.refs_4_ = bf16[896,128]{1,0:T(8,128)(2,1)} collective-permute-done((bf16[896,128]{1,0:T(8,128)(2,1)}, bf16[896,128]{1,0:T(8,128)(2,1)}, u32[]{:S(2)}, u32[]{:S(2)}) %collective-permute-start.2) | collective-permute-done | bytes 229408 | tf_op jit(solution)/shard_map/ppermute | solution.py:28
  39.2 0.0 all-gather.2.cloned.1.call-update
  39.3 0.1 collective-permute-start.12
  39.4 0.8 pad_add_fusion.coords_ref
  40.1 5.5 %collective-permute-done.12.refs_6_ = bf16[896,128]{1,0:T(8,128)(2,1)S(1)} collective-permute-done((bf16[896,128]{1,0:T(8,128)(2,1)}, bf16[896,128]{1,0:T(8,128)(2,1)S(1)}, u32[]{:S(2)}, u32[]{:S(2)}) %collective-permute-start.12) | collective-permute-done | bytes 229408 | tf_op jit(solution)/shard_map/ppermute | solution.py:28
  45.7 0.7 copy-done.15
  46.4 8.7 %shard_map.163 = (bf16[4,896,128]{2,1,0:T(8,128)(2,1)}, bf16[4,896,128]{2,1,0:T(8,128)(2,1)}, bf16[608,128]{1,0:T(8,128)(2,1)}, bf16[304,128]{1,0:T(8,128)(2,1)}) custom-call(s32[2]{0:T(128)} %pad_add_fusion.coords_ref, bf16[896,128]{1,0:T(8,128)(2,1)} %copy-done.12, bf16[896,128]{1,0:T(8,128)(2,1)} %copy-done.13, ...), custom_call_target="tpu_custom_call" | custom-call | flops 1 | bytes 24500000 | tf_op jit(solution)/shard_map/pallas_call | solution.py:226
  55.1 4.2 %collective-permute-start.13 = (bf16[4,896,128]{2,1,0:T(8,128)(2,1)}, bf16[4,896,128]{2,1,0:T(8,128)(2,1)S(1)}, u32[]{:S(2)}, u32[]{:S(2)}) collective-permute-start(bf16[4,896,128]{2,1,0:T(8,128)(2,1)} %get-tuple-element.40), channel_id=1, source_target_pairs={{0,128},{128,0},{1,129},{129,1},{2,130},{130,2},{3,131},{131,3},{4... | collective-permute-start | bytes 2752520 | tf_op jit(solution)/shard_map/ppermute | solution.py:23
  59.3 0.1 collective-permute-start.14
  59.4 0.4 collective-permute-start.15
  59.8 2.1 %collective-permute-done.15.hidden_arrived_ref = bf16[304,128]{1,0:T(8,128)(2,1)S(1)} collective-permute-done((bf16[304,128]{1,0:T(8,128)(2,1)}, bf16[304,128]{1,0:T(8,128)(2,1)S(1)}, u32[]{:S(2)}, u32[]{:S(2)}) %collective-permute-start.15) | collective-permute-done | bytes 77856 | tf_op jit(solution)/shard_map/ppermute | solution.py:23
  62.0 0.6 copy-done.17
  62.6 0.0 copy-done.16
  62.6 0.4 copy-done.11
  63.0 4.5 %shard_map.164 = bf16[16,800,128]{2,1,0:T(8,128)(2,1)} custom-call(bf16[4,896,128]{2,1,0:T(8,128)(2,1)} %get-tuple-element.39.own_ref, bf16[4,896,128]{2,1,0:T(8,128)(2,1)} %copy-done.11, bf16[608,128]{1,0:T(8,128)(2,1)} %get-tuple-element.41.backs_ref, bf16[608,128]{1,0:T(8,128)(2,1)} %copy-done.16, bf16[304,128]{1,0:T(8,128)(2,1)} %get-tuple-element.42.hidden_ref, ...), custom_call_target="tpu_custom_call" | custom-call | flops 1 | bytes 17500000 | tf_op jit(solution)/shard_map/pallas_call | solution.py:303
  67.6 6.7 %all-to-all-start.1 = ((bf16[16,800,128]{2,1,0:T(8,128)(2,1)}), bf16[16,800,128]{2,1,0:T(8,128)(2,1)S(1)}, u32[]{:S(2)}, u32[]{:S(2)}) async-start(bf16[16,800,128]{2,1,0:T(8,128)(2,1)} %shard_map.164), calls=%async_computation.1 | async-start | bytes 6553600 | tf_op jit(solution)/shard_map/all_to_all | solution.py:644
  74.3 0.9 collective-permute-start.10
  75.2 0.1 collective-permute-start.11
  75.3 0.4 collective-permute-start.9
  75.7 2.2 %collective-permute-done.10.up_other_ref = bf16[304,1792]{1,0:T(8,128)(2,1)} collective-permute-done((bf16[304,1792]{1,0:T(8,128)(2,1)}, bf16[304,1792]{1,0:T(8,128)(2,1)}, u32[]{:S(2)}, u32[]{:S(2)}) %collective-permute-start.10) | collective-permute-done | bytes 1089568 | tf_op jit(solution)/shard_map/ppermute | solution.py:23
  77.9 1.6 collective-permute-done.11.down_other_ref
  79.4 1.6 collective-permute-done.9.gate_other_ref
  81.0 20.2 %all-gather.2.cloned.1.call-done.slices_ref = bf16[8,256,1152]{2,1,0:T(8,128)(2,1)} async-done(((bf16[1,256,1152]{2,1,0:T(8,128)(2,1)}), bf16[8,256,1152]{2,1,0:T(8,128)(2,1)}) %all-gather.2.cloned.1.call-update) | async-done | bytes 4718608 | tf_op jit(solution)/shard_map/all_gather | solution.py:628
  101.2 17.0 %shard_map.162 = (bf16[320,3584]{1,0:T(8,128)(2,1)}, bf16[320,3584]{1,0:T(8,128)(2,1)}, bf16[256,4608]{1,0:T(8,128)(2,1)}, bf16[320,304]{1,0:T(8,128)(2,1)}, bf16[320,608]{1,0:T(8,128)(2,1)}) custom-call(s32[2]{0:T(128)} %pad_add_fusion.coords_ref, bf16[8,256,1152]{2,1,0:T(8,128)(2,1)} %all-gather.2.cloned.1.call-done.slices_ref, ...), custom_call_target="tpu_custom_call" | custom-call | flops 1 | bytes 56000000 | tf_op jit(solution)/shard_map/pallas_call | solution.py:473
  118.2 1.7 copy-done.1
  119.9 10.2 %all-to-all-start.2 = ((bf16[16,16,4608]{2,1,0:T(8,128)(2,1)}), bf16[16,16,4608]{2,1,0:T(8,128)(2,1)S(1)}, u32[]{:S(2)}, u32[]{:S(2)}) async-start(bf16[16,16,4608]{2,1,0:T(8,128)(2,1)} %bitcast.58), calls=%async_computation.2 | async-start | bytes 4718592 | tf_op jit(solution)/shard_map/all_to_all | solution.py:661
  130.2 4.1 %convolution_convert_fusion = bf16[608,1792]{1,0:T(8,128)(2,1)} fusion(bf16[320,608]{1,0:T(8,128)(2,1)} %get-tuple-element.46, bf16[320,3584]{1,0:T(8,128)(2,1)} %get-tuple-element.47, s32[]{:T(128)S(6)} %select_n.9), kind=kOutput, calls=%fused_computation.1 | convolution fusion | flops 698392576 | bytes 3735556 | tf_op jit(solution)/shard_map/sh,sd->hd/dot_general | solution.py:19
  134.3 2.1 %collective-permute-start.16 = (bf16[608,1792]{1,0:T(8,128)(2,1)}, bf16[608,1792]{1,0:T(8,128)(2,1)}, u32[]{:S(2)}, u32[]{:S(2)}) collective-permute-start(bf16[608,1792]{1,0:T(8,128)(2,1)} %convolution_convert_fusion), channel_id=1, source_target_pairs={{0,128},{128,0},{1,129},{129,1},{2,130},{130,2},{3,131},{131,3},{4... | collective-permute-start | bytes 6537224 | tf_op jit(solution)/shard_map/ppermute | solution.py:23
  136.4 0.6 fusion.8
  137.0 1.5 convolution_add_fusion.1.dense_other_ref
  138.5 0.2 copy-done.19
  138.8 0.2 copy-done.21
  138.9 1.7 convolution_convert_fusion.1
  140.7 0.6 collective-permute-start.17
  141.3 0.6 fusion.10
  141.9 1.5 convolution_add_fusion.2.dense_own_ref
  143.4 15.5 %all-to-all-done.2 = bf16[16,16,4608]{2,1,0:T(8,128)(2,1)S(1)} async-done(((bf16[16,16,4608]{2,1,0:T(8,128)(2,1)}), bf16[16,16,4608]{2,1,0:T(8,128)(2,1)S(1)}, u32[]{:S(2)}, u32[]{:S(2)}) %all-to-all-start.2) | async-done | bytes 2359328 | tf_op jit(solution)/shard_map/all_to_all | solution.py:661
  159.0 1.4 copy-done
  160.4 6.4 %shard_map.165 = bf16[8,464,128]{2,1,0:T(8,128)(2,1)} custom-call(s32[2]{0:T(128)} %pad_add_fusion.coords_ref, bf16[256,4608]{1,0:T(8,128)(2,1)} %bitcast.49, bf16[256,4608]{1,0:T(8,128)(2,1)} %bitcast.50, bf16[256,4608]{1,0:T(8,128)(2,1)} %bitcast.51, s32[128,4]{1,0:T(8,128)} %get-tuple-element.44.places_ref, ...), custom_call_target="tpu_custom_call" | custom-call | flops 1 | bytes 21000000 | tf_op jit(solution)/shard_map/pallas_call | solution.py:562
  166.8 4.4 %all-to-all-start.3 = ((bf16[8,464,128]{2,1,0:T(8,128)(2,1)}), bf16[8,464,128]{2,1,0:T(8,128)(2,1)S(1)}, u32[]{:S(2)}, u32[]{:S(2)}) async-start(bf16[8,464,128]{2,1,0:T(8,128)(2,1)} %shard_map.165), calls=%async_computation.3 | async-start | bytes 1900544 | tf_op jit(solution)/shard_map/all_to_all | solution.py:684
  171.2 2.4 %reduce_sum.22 = bf16[800,128]{1,0:T(8,128)(2,1)S(1)} reduce(bf16[16,800,128]{2,1,0:T(8,128)(2,1)} %copy-done.1, bf16[]{:T(256)} %constant.6.clone.1), dimensions={0}, to_apply=%region_1.0 | reduce | flops 1536000 | bytes 3481602 | tf_op jit(solution)/shard_map/reduce_sum | solution.py:656
  173.6 0.2 copy.19
  173.8 0.7 fusion.7
  174.5 0.0 copy-done.22
  174.5 3.2 %fusion.1 = bf16[1,304,1792]{2,1,0:T(8,128)(2,1)} fusion(bf16[320,304]{1,0:T(8,128)(2,1)S(1)} %copy-done.22, bf16[304,1792]{1,0:T(8,128)(2,1)S(1)} %collective-permute-done.17, bf16[320,3584]{1,0:T(8,128)(2,1)} %get-tuple-element.49, s32[]{:T(128)S(6)} %select_n.8), kind=kOutput, calls=%fused_computation.5 | convolution fusion | flops 350285824 | bytes 3520516 | tf_op jit(solution)/shard_map/sh,sd->hd/dot_general | solution.py:19
  177.7 3.0 %add_convert_fusion = bf16[608,1792]{1,0:T(8,128)(2,1)S(1)} fusion(bf16[608,1792]{1,0:T(8,128)(2,1)} %collective-permute-done.16, bf16[320,608]{1,0:T(8,128)(2,1)S(1)} %copy-done.20, bf16[320,3584]{1,0:T(8,128)(2,1)S(1)} %copy-done.18, s32[]{:T(128)S(6)} %select_n.8), kind=kOutput, calls=%fused_computation | convolution fusion | flops 700571648 | bytes 5914628 | tf_op jit(solution)/shard_map/sh,sd->hd/dot_general | solution.py:19
  180.7 1.5 slice_bitcast_fusion
  182.1 16.1 %all-to-all-done.3 = bf16[8,464,128]{2,1,0:T(8,128)(2,1)S(1)} async-done(((bf16[8,464,128]{2,1,0:T(8,128)(2,1)}), bf16[8,464,128]{2,1,0:T(8,128)(2,1)S(1)}, u32[]{:S(2)}, u32[]{:S(2)}) %all-to-all-start.3) | async-done | bytes 950304 | tf_op jit(solution)/shard_map/all_to_all | solution.py:684
  198.2 0.1 convert_reduce_fusion
  198.4 0.7 fusion.6
  199.0 0.6 fusion.14
  (53 shorter events, 0.1 us)
Async XLA Ops:
  7.2 32.0 %collective-permute-start.6 = (bf16[304,1792]{1,0:T(8,128)(2,1)}, bf16[304,1792]{1,0:T(8,128)(2,1)S(1)}, u32[]{:S(2)}, u32[]{:S(2)}) collective-permute-start(bf16[304,1792]{1,0:T(8,128)(2,1)} %bitcast.52), channel_id=1, source_target_pairs={{0,128},{128,0},{1,129},{129,1},{2,130},{130,2},{3,131},{131,3},{4... | collective-permute-start | bytes 3268616 | tf_op jit(solution)/shard_map/ppermute | solution.py:23
  7.9 31.3 %collective-permute-start.7 = (bf16[304,1792]{1,0:T(8,128)(2,1)}, bf16[304,1792]{1,0:T(8,128)(2,1)S(1)}, u32[]{:S(2)}, u32[]{:S(2)}) collective-permute-start(bf16[304,1792]{1,0:T(8,128)(2,1)} %bitcast.55), channel_id=1, source_target_pairs={{0,128},{128,0},{1,129},{129,1},{2,130},{130,2},{3,131},{131,3},{4... | collective-permute-start | bytes 3268616 | tf_op jit(solution)/shard_map/ppermute | solution.py:23
  8.0 31.2 %collective-permute-start.8 = (bf16[304,1792]{1,0:T(8,128)(2,1)}, bf16[304,1792]{1,0:T(8,128)(2,1)}, u32[]{:S(2)}, u32[]{:S(2)}) collective-permute-start(bf16[304,1792]{1,0:T(8,128)(2,1)} %refs_12_), channel_id=1, source_target_pairs={{0,128},{128,0},{1,129},{129,1},{2,130},{130,2},{3,131},{131,3},{4... | collective-permute-start | bytes 3268616 | tf_op jit(solution)/shard_map/ppermute | solution.py:23
  9.4 5.8 %copy-start.9 = (bf16[896,128]{1,0:T(8,128)(2,1)}, bf16[896,128]{1,0:T(8,128)(2,1)S(1)}, u32[]{:S(2)}) copy-start(bf16[896,128]{1,0:T(8,128)(2,1)S(1)} %pad_maximum_fusion.both_ref.refs_7_) | copy-start | bytes 688132
  9.4 15.4 %collective-permute-start = (bf16[896,128]{1,0:T(8,128)(2,1)S(1)}, bf16[896,128]{1,0:T(8,128)(2,1)S(1)}, u32[]{:S(2)}, u32[]{:S(2)}) collective-permute-start(bf16[896,128]{1,0:T(8,128)(2,1)S(1)} %pad_maximum_fusion.both_ref.refs_7_), channel_id=1, source_target_pairs={{0,1},{1,2},{2,3},{3,4},{4,5},{5,6},{6,7},{7,0},{8,9},{9,10},{10,1... | collective-permute-start | bytes 688136 | tf_op jit(solution)/shard_map/ppermute | solution.py:28
  11.2 13.7 %collective-permute-start.3 = (bf16[896,128]{1,0:T(8,128)(2,1)S(1)}, bf16[896,128]{1,0:T(8,128)(2,1)S(1)}, u32[]{:S(2)}, u32[]{:S(2)}) collective-permute-start(bf16[896,128]{1,0:T(8,128)(2,1)S(1)} %pad_maximum_fusion.both_ref.refs_7_), channel_id=1, source_target_pairs={{0,7},{1,0},{2,1},{3,2},{4,3},{5,4},{6,5},{7,6},{8,15},{9,8},{10,9... | collective-permute-start | bytes 688136 | tf_op jit(solution)/shard_map/ppermute | solution.py:28
  18.1 17.0 %all-to-all-start = ((bf16[16,16,1152]{2,1,0:T(8,128)(2,1)}), bf16[16,16,1152]{2,1,0:T(8,128)(2,1)S(1)}, u32[]{:S(2)}, u32[]{:S(2)}) async-start(bf16[16,16,1152]{2,1,0:T(8,128)(2,1)} %bitcast.68), calls=%async_computation | async-start | bytes 1179648 | tf_op jit(solution)/shard_map/all_to_all | solution.py:622
  24.7 76.4 %all-gather.2.cloned.1.call-start = ((), (), s32[]{:S(2)}) async-start(), calls=%async_computation.4 | async-start | bytes 5308416 | tf_op jit(solution)/shard_map/all_gather | solution.py:628
  24.8 20.8 %copy-start.12 = (bf16[896,128]{1,0:T(8,128)(2,1)}, bf16[896,128]{1,0:T(8,128)(2,1)S(1)}, u32[]{:S(2)}) copy-start(bf16[896,128]{1,0:T(8,128)(2,1)S(1)} %collective-permute-done.refs_0_) | copy-start | bytes 688132
  24.8 7.6 %collective-permute-start.1 = (bf16[896,128]{1,0:T(8,128)(2,1)S(1)}, bf16[896,128]{1,0:T(8,128)(2,1)}, u32[]{:S(2)}, u32[]{:S(2)}) collective-permute-start(bf16[896,128]{1,0:T(8,128)(2,1)S(1)} %collective-permute-done.refs_0_), channel_id=1, source_target_pairs={{0,1},{1,2},{2,3},{3,4},{4,5},{5,6},{6,7},{7,0},{8,9},{9,10},{10,1... | collective-permute-start | bytes 688136 | tf_op jit(solution)/shard_map/ppermute | solution.py:28
  24.9 20.7 %copy-start.13 = (bf16[896,128]{1,0:T(8,128)(2,1)}, bf16[896,128]{1,0:T(8,128)(2,1)S(1)}, u32[]{:S(2)}) copy-start(bf16[896,128]{1,0:T(8,128)(2,1)S(1)} %collective-permute-done.3.refs_1_) | copy-start | bytes 688132
  24.9 7.5 %collective-permute-start.4 = (bf16[896,128]{1,0:T(8,128)(2,1)S(1)}, bf16[896,128]{1,0:T(8,128)(2,1)S(1)}, u32[]{:S(2)}, u32[]{:S(2)}) collective-permute-start(bf16[896,128]{1,0:T(8,128)(2,1)S(1)} %collective-permute-done.3.refs_1_), channel_id=1, source_target_pairs={{0,7},{1,0},{2,1},{3,2},{4,3},{5,4},{6,5},{7,6},{8,15},{9,8},{10,9... | collective-permute-start | bytes 688136 | tf_op jit(solution)/shard_map/ppermute | solution.py:28
  32.4 6.8 %collective-permute-start.2 = (bf16[896,128]{1,0:T(8,128)(2,1)}, bf16[896,128]{1,0:T(8,128)(2,1)}, u32[]{:S(2)}, u32[]{:S(2)}) collective-permute-start(bf16[896,128]{1,0:T(8,128)(2,1)} %collective-permute-done.1.refs_2_), channel_id=1, source_target_pairs={{0,1},{1,2},{2,3},{3,4},{4,5},{5,6},{6,7},{7,0},{8,9},{9,10},{10,1... | collective-permute-start | bytes 688136 | tf_op jit(solution)/shard_map/ppermute | solution.py:28
  32.4 13.2 %copy-start.14 = (bf16[896,128]{1,0:T(8,128)(2,1)}, bf16[896,128]{1,0:T(8,128)(2,1)S(1)}, u32[]{:S(2)}) copy-start(bf16[896,128]{1,0:T(8,128)(2,1)S(1)} %collective-permute-done.4.refs_3_) | copy-start | bytes 688132
  32.4 6.8 %collective-permute-start.5 = (bf16[896,128]{1,0:T(8,128)(2,1)S(1)}, bf16[896,128]{1,0:T(8,128)(2,1)}, u32[]{:S(2)}, u32[]{:S(2)}) collective-permute-start(bf16[896,128]{1,0:T(8,128)(2,1)S(1)} %collective-permute-done.4.refs_3_), channel_id=1, source_target_pairs={{0,7},{1,0},{2,1},{3,2},{4,3},{5,4},{6,5},{7,6},{8,15},{9,8},{10,9... | collective-permute-start | bytes 688136 | tf_op jit(solution)/shard_map/ppermute | solution.py:28
  35.1 4.2 %copy-start.8 = (bf16[16,16,1152]{2,1,0:T(8,128)(2,1)}, bf16[16,16,1152]{2,1,0:T(8,128)(2,1)S(1)}, u32[]{:S(2)}) copy-start(bf16[16,16,1152]{2,1,0:T(8,128)(2,1)S(1)} %all-to-all-done) | copy-start | bytes 1769476
  39.2 6.5 %copy-start.3 = (bf16[304,1792]{1,0:T(8,128)(2,1)}, bf16[304,1792]{1,0:T(8,128)(2,1)S(1)}, u32[]{:S(2)}) copy-start(bf16[304,1792]{1,0:T(8,128)(2,1)S(1)} %collective-permute-done.6.refs_9_) | copy-start | bytes 3268612
  39.2 6.5 %copy-start.6 = (bf16[304,1792]{1,0:T(8,128)(2,1)}, bf16[304,1792]{1,0:T(8,128)(2,1)S(1)}, u32[]{:S(2)}) copy-start(bf16[304,1792]{1,0:T(8,128)(2,1)S(1)} %collective-permute-done.7.refs_11_) | copy-start | bytes 3268612
  39.3 6.4 %collective-permute-start.12 = (bf16[896,128]{1,0:T(8,128)(2,1)}, bf16[896,128]{1,0:T(8,128)(2,1)S(1)}, u32[]{:S(2)}, u32[]{:S(2)}) collective-permute-start(bf16[896,128]{1,0:T(8,128)(2,1)} %collective-permute-done.2.refs_4_), channel_id=1, source_target_pairs={{0,1},{1,2},{2,3},{3,4},{4,5},{5,6},{6,7},{7,0},{8,9},{9,10},{10,1... | collective-permute-start | bytes 688136 | tf_op jit(solution)/shard_map/ppermute | solution.py:28
  45.7 0.7 copy-start.15
  55.1 6.8 %collective-permute-start.13 = (bf16[4,896,128]{2,1,0:T(8,128)(2,1)}, bf16[4,896,128]{2,1,0:T(8,128)(2,1)S(1)}, u32[]{:S(2)}, u32[]{:S(2)}) collective-permute-start(bf16[4,896,128]{2,1,0:T(8,128)(2,1)} %get-tuple-element.40), channel_id=1, source_target_pairs={{0,128},{128,0},{1,129},{129,1},{2,130},{130,2},{3,131},{131,3},{4... | collective-permute-start | bytes 2752520 | tf_op jit(solution)/shard_map/ppermute | solution.py:23
  59.3 2.6 %collective-permute-start.14 = (bf16[608,128]{1,0:T(8,128)(2,1)}, bf16[608,128]{1,0:T(8,128)(2,1)S(1)}, u32[]{:S(2)}, u32[]{:S(2)}) collective-permute-start(bf16[608,128]{1,0:T(8,128)(2,1)} %get-tuple-element.41.backs_ref), channel_id=1, source_target_pairs={{0,128},{128,0},{1,129},{129,1},{2,130},{130,2},{3,131},{131,3},{4... | collective-permute-start | bytes 466952 | tf_op jit(solution)/shard_map/ppermute | solution.py:23
  59.4 2.5 %collective-permute-start.15 = (bf16[304,128]{1,0:T(8,128)(2,1)}, bf16[304,128]{1,0:T(8,128)(2,1)S(1)}, u32[]{:S(2)}, u32[]{:S(2)}) collective-permute-start(bf16[304,128]{1,0:T(8,128)(2,1)} %get-tuple-element.42.hidden_ref), channel_id=1, source_target_pairs={{0,128},{128,0},{1,129},{129,1},{2,130},{130,2},{3,131},{131,3},{4... | collective-permute-start | bytes 233480 | tf_op jit(solution)/shard_map/ppermute | solution.py:23
  62.0 0.6 copy-start.17
  62.0 0.7 copy-start.16
  62.0 1.1 copy-start.11
  67.6 50.6 %all-to-all-start.1 = ((bf16[16,800,128]{2,1,0:T(8,128)(2,1)}), bf16[16,800,128]{2,1,0:T(8,128)(2,1)S(1)}, u32[]{:S(2)}, u32[]{:S(2)}) async-start(bf16[16,800,128]{2,1,0:T(8,128)(2,1)} %shard_map.164), calls=%async_computation.1 | async-start | bytes 6553600 | tf_op jit(solution)/shard_map/all_to_all | solution.py:644
  74.3 3.6 %collective-permute-start.10 = (bf16[304,1792]{1,0:T(8,128)(2,1)}, bf16[304,1792]{1,0:T(8,128)(2,1)}, u32[]{:S(2)}, u32[]{:S(2)}) collective-permute-start(bf16[304,1792]{1,0:T(8,128)(2,1)} %bitcast.63), channel_id=1, source_target_pairs={{0,128},{128,0},{1,129},{129,1},{2,130},{130,2},{3,131},{131,3},{4... | collective-permute-start | bytes 3268616 | tf_op jit(solution)/shard_map/ppermute | solution.py:23
  75.2 4.2 %collective-permute-start.11 = (bf16[304,1792]{1,0:T(8,128)(2,1)}, bf16[304,1792]{1,0:T(8,128)(2,1)}, u32[]{:S(2)}, u32[]{:S(2)}) collective-permute-start(bf16[304,1792]{1,0:T(8,128)(2,1)} %bitcast.65), channel_id=1, source_target_pairs={{0,128},{128,0},{1,129},{129,1},{2,130},{130,2},{3,131},{131,3},{4... | collective-permute-start | bytes 3268616 | tf_op jit(solution)/shard_map/ppermute | solution.py:23
  75.3 5.7 %collective-permute-start.9 = (bf16[304,1792]{1,0:T(8,128)(2,1)}, bf16[304,1792]{1,0:T(8,128)(2,1)}, u32[]{:S(2)}, u32[]{:S(2)}) collective-permute-start(bf16[304,1792]{1,0:T(8,128)(2,1)} %bitcast.61), channel_id=1, source_target_pairs={{0,128},{128,0},{1,129},{129,1},{2,130},{130,2},{3,131},{131,3},{4... | collective-permute-start | bytes 3268616 | tf_op jit(solution)/shard_map/ppermute | solution.py:23
  118.2 1.7 copy-start.1
  119.9 39.1 %all-to-all-start.2 = ((bf16[16,16,4608]{2,1,0:T(8,128)(2,1)}), bf16[16,16,4608]{2,1,0:T(8,128)(2,1)S(1)}, u32[]{:S(2)}, u32[]{:S(2)}) async-start(bf16[16,16,4608]{2,1,0:T(8,128)(2,1)} %bitcast.58), calls=%async_computation.2 | async-start | bytes 4718592 | tf_op jit(solution)/shard_map/all_to_all | solution.py:661
  130.1 6.2 %copy-start.7 = (bf16[304,1792]{1,0:T(8,128)(2,1)S(1)}, bf16[304,1792]{1,0:T(8,128)(2,1)}, u32[]{:S(2)}) copy-start(bf16[304,1792]{1,0:T(8,128)(2,1)} %copy-done.6) | copy-start | bytes 3268612
  130.2 6.2 %copy-start.10 = (bf16[608,128]{1,0:T(8,128)(2,1)S(1)}, bf16[608,128]{1,0:T(8,128)(2,1)}, u32[]{:S(2)}) copy-start(bf16[608,128]{1,0:T(8,128)(2,1)} %get-tuple-element.41.backs_ref) | copy-start | bytes 466948
  134.3 2.7 %copy-start.4 = (bf16[304,1792]{1,0:T(8,128)(2,1)S(1)}, bf16[304,1792]{1,0:T(8,128)(2,1)}, u32[]{:S(2)}) copy-start(bf16[304,1792]{1,0:T(8,128)(2,1)} %copy-done.3) | copy-start | bytes 3268612
  134.3 43.4 %collective-permute-start.16 = (bf16[608,1792]{1,0:T(8,128)(2,1)}, bf16[608,1792]{1,0:T(8,128)(2,1)}, u32[]{:S(2)}, u32[]{:S(2)}) collective-permute-start(bf16[608,1792]{1,0:T(8,128)(2,1)} %convolution_convert_fusion), channel_id=1, source_target_pairs={{0,128},{128,0},{1,129},{129,1},{2,130},{130,2},{3,131},{131,3},{4... | collective-permute-start | bytes 6537224 | tf_op jit(solution)/shard_map/ppermute | solution.py:23
  137.0 1.8 copy-start.19
  137.0 2.0 copy-start.21
  138.9 2.4 %copy-start.5 = (bf16[1792,304]{0,1:T(8,128)(2,1)S(1)}, bf16[1792,304]{0,1:T(8,128)(2,1)}, u32[]{:S(2)}) copy-start(bf16[1792,304]{0,1:T(8,128)(2,1)} %param.15) | copy-start | bytes 3268612
  140.7 1.2 copy-start.2
  140.7 33.8 %collective-permute-start.17 = (bf16[304,1792]{1,0:T(8,128)(2,1)}, bf16[304,1792]{1,0:T(8,128)(2,1)S(1)}, u32[]{:S(2)}, u32[]{:S(2)}) collective-permute-start(bf16[304,1792]{1,0:T(8,128)(2,1)} %convolution_convert_fusion.1), channel_id=1, source_target_pairs={{0,128},{128,0},{1,129},{129,1},{2,130},{130,2},{3,131},{131,3},{4... | collective-permute-start | bytes 3268616 | tf_op jit(solution)/shard_map/ppermute | solution.py:23
  159.0 1.4 copy-start
  166.8 31.5 %all-to-all-start.3 = ((bf16[8,464,128]{2,1,0:T(8,128)(2,1)}), bf16[8,464,128]{2,1,0:T(8,128)(2,1)S(1)}, u32[]{:S(2)}, u32[]{:S(2)}) async-start(bf16[8,464,128]{2,1,0:T(8,128)(2,1)} %shard_map.165), calls=%async_computation.3 | async-start | bytes 1900544 | tf_op jit(solution)/shard_map/all_to_all | solution.py:684
  173.6 0.9 copy-start.22
  174.5 3.2 %copy-start.18 = (bf16[320,3584]{1,0:T(8,128)(2,1)S(1)}, bf16[320,3584]{1,0:T(8,128)(2,1)}, u32[]{:S(2)}) copy-start(bf16[320,3584]{1,0:T(8,128)(2,1)} %get-tuple-element.47) | copy-start | bytes 6881284
  174.5 3.2 %copy-start.20 = (bf16[320,608]{1,0:T(8,128)(2,1)S(1)}, bf16[320,608]{1,0:T(8,128)(2,1)}, u32[]{:S(2)}) copy-start(bf16[320,608]{1,0:T(8,128)(2,1)} %get-tuple-element.46) | copy-start | bytes 1167364
Sparse Core Ops, SparseCore 0:
  39.4 61.7 all-gather.1
